TPU v7x, 32 devices: a whole 2x2x4 slice. The times are simulated.
32 devices in a mesh: gx: 2 (over y), gy: 4 (over x, core), gz: 4 (over z).
Axes of the slice: x: 2, y: 2, z: 4, core: 2. Of those that a mesh axis runs over, the one named last changes fastest.
Arguments:
- node_feat: float32 [16384, 128], P(('gx', 'gy', 'gz')), may hold values from -6 to 6
- edge_feat: float32 [65536, 128], P(('gx', 'gy', 'gz')), may hold values from -6 to 6
- node_cot: float32 [16384, 128], P(('gx', 'gy', 'gz')), may hold values from -6 to 6
- edge_cot: float32 [65536, 128], P(('gx', 'gy', 'gz')), may hold values from -6 to 6
- sender: int32 [65536], P(('gx', 'gy', 'gz')), may hold values from 0 to 1375, as said below
- receiver: int32 [65536], P(('gx', 'gy', 'gz')), may hold values from 0 to 511, as said below
- block_count: int32 [512], P(('gx', 'gy', 'gz')), may hold values from 0 to 128, as said below
- send_rows: int32 [6, 12, 12, 32], P('gx', 'gy', 'gz'), may hold values from 0 to 511, as said below
- edge_in_weight: float32 [384, 128], replicated, may hold values from -0.3125 to 0.3125
- edge_bias: float32 [128], replicated, may hold values from -3 to 3
- edge_out_weight: float32 [128, 128], replicated, may hold values from -0.5 to 0.5
- edge_gain: float32 [128], replicated, may hold values from 0.1 to 1.9
- node_in_weight: float32 [256, 128], replicated, may hold values from -0.375 to 0.375
- node_bias: float32 [128], replicated, may hold values from -3 to 3
- node_out_weight: float32 [128, 128], replicated, may hold values from -0.5 to 0.5
- node_gain: float32 [128], replicated, may hold values from 0.1 to 1.9
Outputs:
- node_grad: float32 [16384, 128], P(('gx', 'gy', 'gz'))
- edge_grad: float32 [65536, 128], P(('gx', 'gy', 'gz'))
- edge_in_grad: float32 [384, 128], replicated
- edge_bias_grad: float32 [128], replicated
- edge_out_grad: float32 [128, 128], replicated
- edge_gain_grad: float32 [128], replicated
- node_in_grad: float32 [256, 128], replicated
- node_bias_grad: float32 [128], replicated
- node_out_grad: float32 [128, 128], replicated
- node_gain_grad: float32 [128], replicated
Inputs may be any that keep to these rules, and one draw needn't show every extreme that they name: `sender`: A value below 512 is an owned cell; otherwise it is 512 + 32 index(d) + s with s below 32, a halo slot of direction d. It never names direction 13 nor a direction whose neighbour lies outside the device grid. `receiver`: nondecreasing over the edge rows of one device. `block_count`: the nonzero blocks of a device come first; some device has no empty block. `send_rows`: the 32 cells of one list are distinct.
All inputs are finite; a program needn't handle non-finite values.
Results may differ from a plain program's by a relative error of at most 0.000088.
Values sent between devices are 32-bit elements; how exact they have to be, the bound alone decides.
A program may use at most 64 MiB of HBM per device.

v0:
```python
import math

import jax
import jax.numpy as jnp
from jax import lax
from jax.sharding import PartitionSpec as P

NORM_EPS = 1e-05
HIGHEST = lax.Precision.HIGHEST


def with_halo(value, sides, width):
    for axis, dim in sides:
        peers, length = (lax.axis_size(axis), value.shape[dim])
        up = [(i, (i + 1) % peers) for i in range(peers - 1)]
        down = [(j, i) for i, j in up]
        last = lax.slice_in_dim(value, length - width, length, axis=dim)
        initial = lax.slice_in_dim(value, 0, width, axis=dim)
        before = lax.ppermute(last, axis, up)
        after = lax.ppermute(initial, axis, down)
        value = jnp.concatenate([before, value, after], axis=dim)
    return value


def layer_norm(values, gain):
    average = jnp.mean(values, axis=-1, keepdims=True)
    centred = values - average
    spread_sq = jnp.mean(centred * centred, axis=-1, keepdims=True)
    return centred * lax.rsqrt(spread_sq + NORM_EPS) * gain


def edge_section(
    node_table,
    edge_feat,
    sender,
    receiver,
    valid_mask,
    edge_in_weight,
    edge_bias,
    edge_out_weight,
    edge_gain,
):
    width = edge_feat.shape[1]
    preact = jnp.dot(edge_feat, edge_in_weight[:width], precision=HIGHEST)
    preact = preact + jnp.dot(
        node_table[sender], edge_in_weight[width : 2 * width], precision=HIGHEST
    )
    preact = preact + jnp.dot(node_table[receiver], edge_in_weight[2 * width :], precision=HIGHEST)
    hidden = jax.nn.silu(preact + edge_bias)
    return (
        layer_norm(jnp.dot(hidden, edge_out_weight, precision=HIGHEST), edge_gain)
        * valid_mask[:, None]
    )


def node_section(node_feat, summed, node_in_weight, node_bias, node_out_weight, node_gain):
    width = node_feat.shape[1]
    preact = jnp.dot(node_feat, node_in_weight[:width], precision=HIGHEST) + jnp.dot(
        summed, node_in_weight[width:], precision=HIGHEST
    )
    hidden = jax.nn.silu(preact + node_bias)
    return node_feat + layer_norm(jnp.dot(hidden, node_out_weight, precision=HIGHEST), node_gain)


def outer_directions():
    index = lax.broadcasted_iota(jnp.int32, (27,), 0)
    return (index != 13).astype(jnp.float32).reshape(3, 3, 3, 1, 1)


def share_rows(packets):
    spread = with_halo(packets, (("gx", 0), ("gy", 1), ("gz", 2)), 1)
    return spread[::2, ::2, ::2]


def return_grads(slot_grads):
    spread = with_halo(slot_grads, (("gx", 0), ("gy", 1), ("gz", 2)), 1)
    return spread[::2, ::2, ::2]


def on_device(
    node_feat,
    edge_feat,
    node_cot,
    edge_cot,
    sender,
    receiver,
    block_count,
    send_rows,
    edge_in_weight,
    edge_bias,
    edge_out_weight,
    edge_gain,
    node_in_weight,
    node_bias,
    node_out_weight,
    node_gain,
):
    num_cells, width = node_feat.shape
    edge_rows = edge_feat.shape[0]
    slot_count = send_rows.shape[3]
    total_rows = lax.axis_size("gx") * lax.axis_size("gy") * lax.axis_size("gz") * edge_rows
    grad_scale = 1.0 / math.sqrt(total_rows)
    outer_mask = outer_directions()
    packets = node_feat[send_rows] * outer_mask
    received = share_rows(packets)
    node_table = jnp.concatenate([node_feat, received.reshape(27 * slot_count, width)], axis=0)
    valid_mask = (
        (lax.broadcasted_iota(jnp.int32, (block_count.shape[0], 128), 1) < block_count[:, None])
        .astype(jnp.float32)
        .reshape(edge_rows)
    )

    def edge_part(table_in, feat_in, weight_in, bias_in, weight_out, gain_in):
        return edge_section(
            table_in, feat_in, sender, receiver, valid_mask, weight_in, bias_in, weight_out, gain_in
        )

    message, edge_pull = jax.vjp(
        edge_part, node_table, edge_feat, edge_in_weight, edge_bias, edge_out_weight, edge_gain
    )
    summed = jax.ops.segment_sum(message, receiver, num_segments=num_cells, indices_are_sorted=True)
    _, node_pull = jax.vjp(
        node_section, node_feat, summed, node_in_weight, node_bias, node_out_weight, node_gain
    )
    node_grads = node_pull(node_cot)
    node_weights = (node_grads[2], node_grads[3], node_grads[4], node_grads[5])
    edge_grads = edge_pull(edge_cot + node_grads[1][receiver])
    combined = lax.psum(
        (
            edge_grads[2],
            edge_grads[3],
            edge_grads[4],
            edge_grads[5],
            node_weights[0],
            node_weights[1],
            node_weights[2],
            node_weights[3],
        ),
        ("gx", "gy", "gz"),
    )
    edge_weights = combined[:4]
    node_weights = combined[4:]
    table_grad = edge_grads[0]
    slot_grads = table_grad[num_cells:].reshape(3, 3, 3, slot_count, width) * outer_mask
    returned = return_grads(slot_grads) * outer_mask
    halo_sum = jax.ops.segment_sum(
        returned.reshape(27 * slot_count, width),
        send_rows.reshape(27 * slot_count),
        num_segments=num_cells,
    )
    node_grad = node_grads[0] + table_grad[:num_cells] + halo_sum
    edge_grad = edge_cot + edge_grads[1]
    return (
        node_grad,
        edge_grad,
        edge_weights[0] * grad_scale,
        edge_weights[1] * grad_scale,
        edge_weights[2] * grad_scale,
        edge_weights[3] * grad_scale,
        node_weights[0] * grad_scale,
        node_weights[1] * grad_scale,
        node_weights[2] * grad_scale,
        node_weights[3] * grad_scale,
    )


def solution(mesh):
    return jax.shard_map(
        on_device,
        mesh=mesh,
        in_specs=(
            P(("gx", "gy", "gz"), None),
            P(("gx", "gy", "gz"), None),
            P(("gx", "gy", "gz"), None),
            P(("gx", "gy", "gz"), None),
            P(("gx", "gy", "gz")),
            P(("gx", "gy", "gz")),
            P(("gx", "gy", "gz")),
            P("gx", "gy", "gz", None),
            P(),
            P(),
            P(),
            P(),
            P(),
            P(),
            P(),
            P(),
        ),
        out_specs=(
            P(("gx", "gy", "gz"), None),
            P(("gx", "gy", "gz"), None),
            P(),
            P(),
            P(),
            P(),
            P(),
            P(),
            P(),
            P(),
        ),
        check_vma=False,
    )
```

profile of v0, /device:TPU:0, one launch (start us, length us, event | category | flops | bytes accessed | tf_op | source)
XLA Modules:
  0.0 361.0 jit_solution(1524779781735105257)
XLA Ops:
  7.3 0.8 compare_select_fusion
  8.2 2.8 gather_fusion
  11.2 5.0 %collective-permute-start = (f32[1,3,3,32,128]{4,3,2,1,0:T(8,128)S(1)}, f32[1,3,3,32,128]{4,3,2,1,0:T(8,128)S(1)}, u32[]{:S(2)}, u32[]{:S(2)}) collective-permute-start(f32[1,3,3,32,128]{4,3,2,1,0:T(8,128)S(1)} %get-tuple-element.37), channel_id=1, source_target_pairs={{0,16},{1,17},{2,18},{3,19},{4,20},{5,21},{6,22},{7,23},{8,24},{9,... | collective-permute-start | bytes 442376 | tf_op jit(solution)/shard_map/ppermute | solution.py:19
  16.2 1.3 collective-permute-start.1
  18.2 1.2 collective-permute-done
  19.3 4.1 %collective-permute-done.1 = f32[1,3,3,32,128]{4,3,2,1,0:T(8,128)S(1)} collective-permute-done((f32[1,3,3,32,128]{4,3,2,1,0:T(8,128)S(1)}, f32[1,3,3,32,128]{4,3,2,1,0:T(8,128)S(1)}, u32[]{:S(2)}, u32[]{:S(2)}) %collective-permute-start.1) | collective-permute-done | bytes 147488 | tf_op jit(solution)/shard_map/ppermute | solution.py:20
  23.4 0.8 pad_maximum_fusion.18
  24.3 2.0 collective-permute-start.2
  26.3 1.3 collective-permute-start.3
  28.8 0.8 copy.32
  29.7 1.3 copy.34
  31.0 1.9 fusion.47
  32.9 1.1 pad_maximum_fusion.12
  34.0 3.5 collective-permute-start.4
  37.5 1.3 collective-permute-start.5
  38.8 0.7 convert_bitcast_fusion
  39.5 1.9 fusion.44
  41.4 4.1 %collective-permute-done.4 = f32[5,5,1,32,128]{4,3,2,1,0:T(8,128)S(1)} collective-permute-done((f32[5,5,1,32,128]{4,3,2,1,0:T(8,128)S(1)}, f32[5,5,1,32,128]{4,3,2,1,0:T(8,128)S(1)}, u32[]{:S(2)}, u32[]{:S(2)}) %collective-permute-start.4) | collective-permute-done | bytes 409632 | tf_op jit(solution)/shard_map/ppermute | solution.py:19
  45.5 4.7 %collective-permute-done.5 = f32[5,5,1,32,128]{4,3,2,1,0:T(8,128)S(1)} collective-permute-done((f32[5,5,1,32,128]{4,3,2,1,0:T(8,128)S(1)}, f32[5,5,1,32,128]{4,3,2,1,0:T(8,128)S(1)}, u32[]{:S(2)}, u32[]{:S(2)}) %collective-permute-start.5) | collective-permute-done | bytes 409632 | tf_op jit(solution)/shard_map/ppermute | solution.py:20
  50.2 1.2 pad_maximum_fusion
  51.5 5.5 %gather_fusion.1 = f32[2048,128]{1,0:T(8,128)S(1)} fusion(f32[1376,128]{1,0:T(8,128)S(1)} %pad_maximum_fusion.2, s32[2048]{0:T(1024)S(1)} %get-tuple-element.40), kind=kCustom, calls=%fused_computation.1 | custom fusion | bytes 2105344 | tf_op jit(solution)/shard_map/jvp()/gather | solution.py:46
  57.0 7.6 %gather_fusion.2 = f32[2048,128]{1,0:T(8,128)} fusion(f32[1376,128]{1,0:T(8,128)S(1)} %pad_maximum_fusion.2, s32[2048]{0:T(1024)S(1)} %get-tuple-element.42), kind=kCustom, calls=%fused_computation.2 | custom fusion | bytes 2105344 | tf_op jit(solution)/shard_map/jvp()/gather | solution.py:48
  64.6 2.3 convolution_add_fusion.2
  66.9 1.0 fusion
  67.9 1.3 fusion.64
  70.2 1.3 copy.33
  71.5 13.0 %scatter_custom_fusion = f32[512,128]{1,0:T(8,128)S(1)} fusion(s32[2048]{0:T(1024)} %param.21, f32[2048,128]{1,0:T(8,128)} %copy.33, f32[]{:T(128)} %constant.12.clone.1), kind=kCustom, calls=%fused_computation.79 | custom fusion | flops 262144 | bytes 262656 | tf_op jit(solution)/shard_map/scatter-add | solution.py:121
  84.6 1.4 fusion.2
  85.9 1.3 fusion.65
  88.2 1.1 fusion.67
  89.3 1.2 fusion.21
  90.9 1.2 fusion.70
  92.1 1.2 convolution_bitcast_fusion.1
  93.4 8.4 %gather_fusion.3 = f32[2048,128]{1,0:T(8,128)} fusion(f32[512,128]{1,0:T(8,128)S(1)} %fusion.34, s32[2048]{0:T(1024)} %get-tuple-element.41), kind=kCustom, calls=%fused_computation.3 | custom fusion | bytes 2105344 | tf_op jit(solution)/shard_map/gather | solution.py:127
  101.7 2.7 copy.35
  104.4 1.6 multiply_reduce_fusion
  106.4 0.8 copy-done.15
  107.3 1.9 fusion.66
  109.2 2.6 fusion.6
  111.8 2.4 fusion.68
  114.3 2.4 fusion.69
  116.7 2.5 convolution_bitcast_fusion
  119.2 2.0 fusion.40
  121.1 2.2 fusion.37
  123.3 12.0 %scatter_custom_fusion.2 = f32[1376,128]{1,0:T(8,128)S(1)} fusion(s32[2048]{0:T(1024)} %get-tuple-element.39, f32[2048,128]{1,0:T(8,128)} %fusion.40, f32[]{:T(128)} %constant.12.clone.1), kind=kCustom, calls=%fused_computation.51 | custom fusion | flops 262144 | bytes 705024 | tf_op jit(solution)/shard_map/transpose(jvp())/scatter-add | solution.py:46
  135.4 13.6 %scatter_custom_fusion.1 = f32[1376,128]{1,0:T(8,128)} fusion(s32[2048]{0:T(1024)} %get-tuple-element.43, f32[2048,128]{1,0:T(8,128)} %fusion.37, f32[]{:T(128)} %constant.12.clone.1), kind=kCustom, calls=%fused_computation.53 | custom fusion | flops 262144 | bytes 705024 | tf_op jit(solution)/shard_map/transpose(jvp())/scatter-add | solution.py:48
  148.9 1.3 add_any.50
  150.3 1.4 fusion.1
  151.7 2.0 convolution_add_fusion
  153.8 1.4 collective-permute-start.6
  155.2 1.3 collective-permute-start.7
  157.2 0.7 pad_add_fusion
  157.9 43.6 %all-reduce.5 = (f32[128]{0:T(128)S(1)}, f32[128]{0:T(128)S(1)}, f32[128]{0:T(128)S(1)}, f32[128]{0:T(128)S(1)}) all-reduce(f32[128]{0:T(128)S(1)} %get-tuple-element.48, f32[128]{0:T(128)S(1)} %get-tuple-element.10, f32[128]{0:T(128)S(1)} %copy-done.43, f32[128]{0:T(128)S(1)} %copy-done.39), channel_id=1, replica_groups=mesh['gx'=2,'gy'=4,'gz'=4] {'gx','gy','gz'}, use_global_device_ids=true, to_apply=%region_14.15 | all-reduce | flops 512 | bytes 4096 | tf_op jit(solution)/shard_map/psum | solution.py:128
  202.1 1.3 collective-permute-start.8
  203.4 1.3 collective-permute-start.9
  205.2 123.6 %all-reduce.9.cloned.1.call-done = (f32[384,128]{1,0:T(8,128)}, f32[128,128]{1,0:T(8,128)}, f32[256,128]{1,0:T(8,128)}, f32[128,128]{1,0:T(8,128)}) async-done(((f32[384,128]{1,0:T(8,128)}, f32[128,128]{1,0:T(8,128)}, f32[256,128]{1,0:T(8,128)}, f32[128,128]{1,0:T(8,128)}), (f32[384,128]{1,0:T(8,128)}, f32[128,128]{1,0:T(8,128)}, f32[256,128]{1,0:T(8,128)}, ...) | async-done | bytes 458768 | tf_op jit(solution)/shard_map/psum | solution.py:128
  328.8 1.6 broadcast_multiply_fusion.3
  330.5 5.3 %collective-permute-start.10 = (f32[5,5,1,32,128]{4,3,2,1,0:T(8,128)S(1)}, f32[5,5,1,32,128]{4,3,2,1,0:T(8,128)S(1)}, u32[]{:S(2)}, u32[]{:S(2)}) collective-permute-start(f32[5,5,1,32,128]{4,3,2,1,0:T(8,128)S(1)} %get-tuple-element.27), channel_id=1, source_target_pairs={{0,1},{1,2},{2,3},{4,5},{5,6},{6,7},{8,9},{9,10},{10,11},{12,13},{... | collective-permute-start | bytes 1228808 | tf_op jit(solution)/shard_map/ppermute | solution.py:19
  335.8 1.3 collective-permute-start.11
  337.8 0.7 broadcast_multiply_fusion.2
  338.4 4.4 %collective-permute-done.10 = f32[5,5,1,32,128]{4,3,2,1,0:T(8,128)S(1)} collective-permute-done((f32[5,5,1,32,128]{4,3,2,1,0:T(8,128)S(1)}, f32[5,5,1,32,128]{4,3,2,1,0:T(8,128)S(1)}, u32[]{:S(2)}, u32[]{:S(2)}) %collective-permute-start.10) | collective-permute-done | bytes 409632 | tf_op jit(solution)/shard_map/ppermute | solution.py:19
  342.8 4.1 %collective-permute-done.11 = f32[5,5,1,32,128]{4,3,2,1,0:T(8,128)S(1)} collective-permute-done((f32[5,5,1,32,128]{4,3,2,1,0:T(8,128)S(1)}, f32[5,5,1,32,128]{4,3,2,1,0:T(8,128)S(1)}, u32[]{:S(2)}, u32[]{:S(2)}) %collective-permute-start.11) | collective-permute-done | bytes 409632 | tf_op jit(solution)/shard_map/ppermute | solution.py:20
  347.2 6.2 %scatter_fusion = f32[512,128]{1,0:T(8,128)S(1)} fusion(f32[512,128]{1,0:T(8,128)S(1)} %fusion.1, s32[864]{0:T(1024)S(1)} %copy-done.34, f32[864,128]{1,0:T(8,128)S(1)} %bitcast.37), kind=kCustom, calls=%fused_computation.7 | custom fusion | flops 110592 | bytes 1330560 | tf_op jit(solution)/shard_map/scatter-add | solution.py:146
  353.4 0.7 copy-done.2
  (138 shorter events, 7.8 us)
Async XLA Ops:
  7.2 32.3 %copy-start = (f32[2048,128]{1,0:T(8,128)S(1)}, f32[2048,128]{1,0:T(8,128)}, u32[]{:S(2)}) copy-start(f32[2048,128]{1,0:T(8,128)} %param.17) | copy-start | bytes 3145732
  7.2 321.6 %all-reduce.9.cloned.1.call-start = ((), (), s32[]{:S(2)}) async-start(), calls=%async_computation | async-start | bytes 917504 | tf_op jit(solution)/shard_map/psum | solution.py:128
  7.2 3.9 %copy-start.25 = (f32[3,3,3]{2,1,0:T(4,128)}, f32[3,3,3]{2,1,0:T(4,128)S(1)}, u32[]{:S(2)}) copy-start(f32[3,3,3]{2,1,0:T(4,128)S(1)} %fusion.54) | copy-start | bytes 328
  8.2 9.4 %copy-start.36 = (s32[2048]{0:T(1024)S(1)}, s32[2048]{0:T(1024)}, u32[]{:S(2)}) copy-start(s32[2048]{0:T(1024)} %param.21) | copy-start | bytes 24580
  11.0 16.5 %copy-start.35 = (s32[2048]{0:T(1024)S(1)}, s32[2048]{0:T(1024)}, u32[]{:S(2)}) copy-start(s32[2048]{0:T(1024)} %param.20) | copy-start | bytes 24580
  11.0 17.1 %copy-start.31 = (s32[3,3,3,32]{3,2,1,0:T(4,128)S(1)}, s32[3,3,3,32]{3,2,1,0:T(4,128)}, u32[]{:S(2)}) copy-start(s32[3,3,3,32]{3,2,1,0:T(4,128)} %param.23) | copy-start | bytes 10372
  11.0 17.8 %copy-start.13 = (f32[512,128]{1,0:T(8,128)S(1)}, f32[512,128]{1,0:T(8,128)}, u32[]{:S(2)}) copy-start(f32[512,128]{1,0:T(8,128)} %param.18) | copy-start | bytes 786436
  11.0 18.6 %copy-start.7 = (f32[2048,128]{1,0:T(8,128)S(1)}, f32[2048,128]{1,0:T(8,128)}, u32[]{:S(2)}) copy-start(f32[2048,128]{1,0:T(8,128)} %param.19) | copy-start | bytes 3145732
  11.2 19.8 %copy-start.1 = (f32[512,128]{1,0:T(8,128)S(1)}, f32[512,128]{1,0:T(8,128)}, u32[]{:S(2)}) copy-start(f32[512,128]{1,0:T(8,128)} %param.16) | copy-start | bytes 786436
  11.2 8.1 %collective-permute-start = (f32[1,3,3,32,128]{4,3,2,1,0:T(8,128)S(1)}, f32[1,3,3,32,128]{4,3,2,1,0:T(8,128)S(1)}, u32[]{:S(2)}, u32[]{:S(2)}) collective-permute-start(f32[1,3,3,32,128]{4,3,2,1,0:T(8,128)S(1)} %get-tuple-element.37), channel_id=1, source_target_pairs={{0,16},{1,17},{2,18},{3,19},{4,20},{5,21},{6,22},{7,23},{8,24},{9,... | collective-permute-start | bytes 442376 | tf_op jit(solution)/shard_map/ppermute | solution.py:19
  16.2 7.2 %collective-permute-start.1 = (f32[1,3,3,32,128]{4,3,2,1,0:T(8,128)S(1)}, f32[1,3,3,32,128]{4,3,2,1,0:T(8,128)S(1)}, u32[]{:S(2)}, u32[]{:S(2)}) collective-permute-start(f32[1,3,3,32,128]{4,3,2,1,0:T(8,128)S(1)} %get-tuple-element.38), channel_id=1, source_target_pairs={{16,0},{17,1},{18,2},{19,3},{20,4},{21,5},{22,6},{23,7},{24,8},{25... | collective-permute-start | bytes 442376 | tf_op jit(solution)/shard_map/ppermute | solution.py:20
  24.3 8.6 %collective-permute-start.2 = (f32[5,1,3,32,128]{4,3,2,1,0:T(8,128)}, f32[5,1,3,32,128]{4,3,2,1,0:T(8,128)}, u32[]{:S(2)}, u32[]{:S(2)}) collective-permute-start(f32[5,1,3,32,128]{4,3,2,1,0:T(8,128)} %get-tuple-element.33), channel_id=1, source_target_pairs={{0,4},{4,8},{8,12},{1,5},{5,9},{9,13},{2,6},{6,10},{10,14},{3,7},{... | collective-permute-start | bytes 737288 | tf_op jit(solution)/shard_map/ppermute | solution.py:19
  26.3 6.6 %collective-permute-start.3 = (f32[5,1,3,32,128]{4,3,2,1,0:T(8,128)}, f32[5,1,3,32,128]{4,3,2,1,0:T(8,128)}, u32[]{:S(2)}, u32[]{:S(2)}) collective-permute-start(f32[5,1,3,32,128]{4,3,2,1,0:T(8,128)} %get-tuple-element.34), channel_id=1, source_target_pairs={{4,0},{8,4},{12,8},{5,1},{9,5},{13,9},{6,2},{10,6},{14,10},{7,3},{... | collective-permute-start | bytes 737288 | tf_op jit(solution)/shard_map/ppermute | solution.py:20
  29.7 9.1 %copy-start.42 = (s32[16]{0:T(128)S(1)}, s32[16]{0:T(128)}, u32[]{:S(2)}) copy-start(s32[16]{0:T(128)} %param.22) | copy-start | bytes 196
  29.7 9.8 %copy-start.16 = (f32[384,128]{1,0:T(8,128)S(1)}, f32[384,128]{1,0:T(8,128)}, u32[]{:S(2)}) copy-start(f32[384,128]{1,0:T(8,128)} %param.24) | copy-start | bytes 589828
  34.0 11.5 %collective-permute-start.4 = (f32[5,5,1,32,128]{4,3,2,1,0:T(8,128)S(1)}, f32[5,5,1,32,128]{4,3,2,1,0:T(8,128)S(1)}, u32[]{:S(2)}, u32[]{:S(2)}) collective-permute-start(f32[5,5,1,32,128]{4,3,2,1,0:T(8,128)S(1)} %get-tuple-element.29), channel_id=1, source_target_pairs={{0,1},{1,2},{2,3},{4,5},{5,6},{6,7},{8,9},{9,10},{10,11},{12,13},{... | collective-permute-start | bytes 1228808 | tf_op jit(solution)/shard_map/ppermute | solution.py:19
  37.5 12.7 %collective-permute-start.5 = (f32[5,5,1,32,128]{4,3,2,1,0:T(8,128)S(1)}, f32[5,5,1,32,128]{4,3,2,1,0:T(8,128)S(1)}, u32[]{:S(2)}, u32[]{:S(2)}) collective-permute-start(f32[5,5,1,32,128]{4,3,2,1,0:T(8,128)S(1)} %get-tuple-element.30), channel_id=1, source_target_pairs={{1,0},{2,1},{3,2},{5,4},{6,5},{7,6},{9,8},{10,9},{11,10},{13,12},{... | collective-permute-start | bytes 1228808 | tf_op jit(solution)/shard_map/ppermute | solution.py:20
  57.0 7.6 %copy-start.3 = (f32[2048,128]{1,0:T(8,128)}, f32[2048,128]{1,0:T(8,128)S(1)}, u32[]{:S(2)}) copy-start(f32[2048,128]{1,0:T(8,128)S(1)} %gather_fusion.1) | copy-start | bytes 3145732
  64.6 2.3 copy-start.5
  64.6 2.3 copy-start.44
  66.9 1.0 copy-start.46
  67.9 1.4 copy-start.14
  67.9 2.1 copy-start.27
  67.9 2.1 copy-start.37
  69.4 0.6 copy-start.29
  70.0 14.5 %copy-start.18 = (f32[256,128]{1,0:T(8,128)S(1)}, f32[256,128]{1,0:T(8,128)}, u32[]{:S(2)}) copy-start(f32[256,128]{1,0:T(8,128)} %param.28) | copy-start | bytes 393220
  71.5 15.8 %copy-start.12 = (f32[512,128]{0,1:T(8,128)S(1)}, f32[512,128]{0,1:T(8,128)}, u32[]{:S(2)}) copy-start(f32[512,128]{0,1:T(8,128)} %copy.32) | copy-start | bytes 786436
  71.5 15.8 %copy-start.40 = (f32[128]{0:T(128)S(1)}, f32[128]{0:T(128)}, u32[]{:S(2)}) copy-start(f32[128]{0:T(128)} %param.31) | copy-start | bytes 1540
  84.5 3.5 copy-start.41
  84.6 3.6 copy-start.45
  89.3 4.1 %copy-start.10 = (f32[512,128]{1,0:T(8,128)}, f32[512,128]{1,0:T(8,128)S(1)}, u32[]{:S(2)}) copy-start(f32[512,128]{1,0:T(8,128)S(1)} %get-tuple-element.51) | copy-start | bytes 786436
  101.7 2.7 copy-start.9
  101.7 2.7 copy-start.28
  101.7 2.7 copy-start.38
  104.4 1.7 copy-start.30
  106.1 1.2 copy-start.15
  106.1 1.2 copy-start.47
  109.2 2.6 copy-start.6
  111.8 2.5 copy-start.4
  114.3 4.9 %copy-start.17 = (f32[384,128]{1,0:T(8,128)S(1)}, f32[384,128]{1,0:T(8,128)}, u32[]{:S(2)}) copy-start(f32[384,128]{1,0:T(8,128)} %param.24) | copy-start | bytes 589828
  123.3 26.9 %copy-start.11 = (f32[512,128]{1,0:T(8,128)S(1)}, f32[512,128]{1,0:T(8,128)}, u32[]{:S(2)}) copy-start(f32[512,128]{1,0:T(8,128)} %copy-done.10) | copy-start | bytes 786436
  148.9 2.7 copy-start.8
  150.2 3.4 copy-start.26
  151.6 4.9 %copy-start.19 = (f32[128,128]{1,0:T(8,128)S(1)}, f32[128,128]{1,0:T(8,128)}, u32[]{:S(2)}) copy-start(f32[128,128]{1,0:T(8,128)} %fusion.70) | copy-start | bytes 196612
  151.7 4.9 %copy-start.20 = (f32[128,128]{1,0:T(8,128)S(1)}, f32[128,128]{1,0:T(8,128)}, u32[]{:S(2)}) copy-start(f32[128,128]{1,0:T(8,128)} %convolution_bitcast_fusion.1) | copy-start | bytes 196612
  151.7 5.5 %copy-start.21 = (f32[128,128]{1,0:T(8,128)S(1)}, f32[128,128]{1,0:T(8,128)}, u32[]{:S(2)}) copy-start(f32[128,128]{1,0:T(8,128)} %fusion.68) | copy-start | bytes 196612
  151.7 5.5 %copy-start.22 = (f32[128,128]{1,0:T(8,128)S(1)}, f32[128,128]{1,0:T(8,128)}, u32[]{:S(2)}) copy-start(f32[128,128]{1,0:T(8,128)} %fusion.69) | copy-start | bytes 196612
  151.7 5.5 %copy-start.23 = (f32[128,128]{1,0:T(8,128)S(1)}, f32[128,128]{1,0:T(8,128)}, u32[]{:S(2)}) copy-start(f32[128,128]{1,0:T(8,128)} %convolution_bitcast_fusion) | copy-start | bytes 196612
  151.7 6.2 %copy-start.39 = (f32[128]{0:T(128)S(1)}, f32[128]{0:T(128)}, u32[]{:S(2)}) copy-start(f32[128]{0:T(128)} %get-tuple-element.12) | copy-start | bytes 1540
  151.7 6.2 %copy-start.43 = (f32[128]{0:T(128)S(1)}, f32[128]{0:T(128)}, u32[]{:S(2)}) copy-start(f32[128]{0:T(128)} %get-tuple-element.50) | copy-start | bytes 1540
  153.8 48.2 %collective-permute-start.6 = (f32[1,3,3,32,128]{4,3,2,1,0:T(8,128)S(1)}, f32[1,3,3,32,128]{4,3,2,1,0:T(8,128)S(1)}, u32[]{:S(2)}, u32[]{:S(2)}) collective-permute-start(f32[1,3,3,32,128]{4,3,2,1,0:T(8,128)S(1)} %get-tuple-element.35), channel_id=1, source_target_pairs={{0,16},{1,17},{2,18},{3,19},{4,20},{5,21},{6,22},{7,23},{8,24},{9,... | collective-permute-start | bytes 442376 | tf_op jit(solution)/shard_map/ppermute | solution.py:19
  155.2 46.8 %collective-permute-start.7 = (f32[1,3,3,32,128]{4,3,2,1,0:T(8,128)S(1)}, f32[1,3,3,32,128]{4,3,2,1,0:T(8,128)S(1)}, u32[]{:S(2)}, u32[]{:S(2)}) collective-permute-start(f32[1,3,3,32,128]{4,3,2,1,0:T(8,128)S(1)} %get-tuple-element.36), channel_id=1, source_target_pairs={{16,0},{17,1},{18,2},{19,3},{20,4},{21,5},{22,6},{23,7},{24,8},{25... | collective-permute-start | bytes 442376 | tf_op jit(solution)/shard_map/ppermute | solution.py:20
  202.1 128.3 %collective-permute-start.8 = (f32[5,1,3,32,128]{4,3,2,1,0:T(8,128)S(1)}, f32[5,1,3,32,128]{4,3,2,1,0:T(8,128)S(1)}, u32[]{:S(2)}, u32[]{:S(2)}) collective-permute-start(f32[5,1,3,32,128]{4,3,2,1,0:T(8,128)S(1)} %get-tuple-element.31), channel_id=1, source_target_pairs={{0,4},{4,8},{8,12},{1,5},{5,9},{9,13},{2,6},{6,10},{10,14},{3,7},{... | collective-permute-start | bytes 737288 | tf_op jit(solution)/shard_map/ppermute | solution.py:19
  203.4 127.0 %collective-permute-start.9 = (f32[5,1,3,32,128]{4,3,2,1,0:T(8,128)S(1)}, f32[5,1,3,32,128]{4,3,2,1,0:T(8,128)S(1)}, u32[]{:S(2)}, u32[]{:S(2)}) collective-permute-start(f32[5,1,3,32,128]{4,3,2,1,0:T(8,128)S(1)} %get-tuple-element.32), channel_id=1, source_target_pairs={{4,0},{8,4},{12,8},{5,1},{9,5},{13,9},{6,2},{10,6},{14,10},{7,3},{... | collective-permute-start | bytes 737288 | tf_op jit(solution)/shard_map/ppermute | solution.py:20
  328.8 8.3 %copy-start.32 = (f32[128,128]{1,0:T(8,128)S(1)}, f32[128,128]{1,0:T(8,128)}, u32[]{:S(2)}) copy-start(f32[128,128]{1,0:T(8,128)} %get-tuple-element.19) | copy-start | bytes 196612
  328.8 8.3 %copy-start.33 = (f32[128,128]{1,0:T(8,128)S(1)}, f32[128,128]{1,0:T(8,128)}, u32[]{:S(2)}) copy-start(f32[128,128]{1,0:T(8,128)} %get-tuple-element.21) | copy-start | bytes 196612
  328.8 9.0 %copy-start.24 = (f32[384,128]{1,0:T(8,128)S(1)}, f32[384,128]{1,0:T(8,128)}, u32[]{:S(2)}) copy-start(f32[384,128]{1,0:T(8,128)} %get-tuple-element.18) | copy-start | bytes 589828
  330.5 12.3 %collective-permute-start.10 = (f32[5,5,1,32,128]{4,3,2,1,0:T(8,128)S(1)}, f32[5,5,1,32,128]{4,3,2,1,0:T(8,128)S(1)}, u32[]{:S(2)}, u32[]{:S(2)}) collective-permute-start(f32[5,5,1,32,128]{4,3,2,1,0:T(8,128)S(1)} %get-tuple-element.27), channel_id=1, source_target_pairs={{0,1},{1,2},{2,3},{4,5},{5,6},{6,7},{8,9},{9,10},{10,11},{12,13},{... | collective-permute-start | bytes 1228808 | tf_op jit(solution)/shard_map/ppermute | solution.py:19
  335.8 11.2 %collective-permute-start.11 = (f32[5,5,1,32,128]{4,3,2,1,0:T(8,128)S(1)}, f32[5,5,1,32,128]{4,3,2,1,0:T(8,128)S(1)}, u32[]{:S(2)}, u32[]{:S(2)}) collective-permute-start(f32[5,5,1,32,128]{4,3,2,1,0:T(8,128)S(1)} %get-tuple-element.28), channel_id=1, source_target_pairs={{1,0},{2,1},{3,2},{5,4},{6,5},{7,6},{9,8},{10,9},{11,10},{13,12},{... | collective-permute-start | bytes 1228808 | tf_op jit(solution)/shard_map/ppermute | solution.py:20
  338.4 8.8 %copy-start.34 = (s32[864]{0:T(1024)S(1)}, s32[864]{0:T(1024)}, u32[]{:S(2)}) copy-start(s32[864]{0:T(1024)} %reshape.187) | copy-start | bytes 10372
  353.4 0.7 copy-start.2
Sparse Core Ops, SparseCore 0:
  201.7 127.0 all-reduce.8
where the time goes:
time: 362 us; the launch traced here: 361 us
  waiting for transfers between devices  146 us (40%)
  other arithmetic  60.9 us (17%)
  blocking collectives  43.6 us (12%)
  matrix products  35.6 us (10%)
  local copies, waits for them, and re-layouts  33.6 us (9%)
  starting transfers between devices  26.3 us (7%)
  between operations  14.8 us (4%)
    psum x1, waiting for transfers between devices, on_device(): lax.psum((edge_grads[2], edge_grads[3], edge_grads[4], edge_grads[5], nod...  124 us
    psum x1, blocking collectives, on_device(): lax.psum((edge_grads[2], edge_grads[3], edge_grads[4], edge_grads[5], nod...  43.6 us
    ppermute x6, starting transfers between devices, with_halo(): before = lax.ppermute(last, axis, up)  18.5 us
    scatter-add x1, other arithmetic, edge_section(): node_table[receiver]  13.6 us
    scatter-add x1, other arithmetic, on_device(): jax.ops.segment_sum(message, receiver, num_segments=num_cells, indices_ar...  13 us
    ppermute x6, waiting for transfers between devices, with_halo(): after = lax.ppermute(initial, axis, down)  13 us
    scatter-add x1, other arithmetic, edge_section(): node_table[sender]  12 us
    gather x2, local copies, waits for them, and re-layouts, on_device(): edge_grads = edge_pull(edge_cot + node_grads[1][receiver])  11 us
  transfers between devices with their start and end apart: 13, of which 7 were waited for; matrix products, arithmetic and copies ran while one was open for 4% of the time, Pallas kernels for 0%

commit v1 on v0

v1 whole, which is shorter than its diff:
```python
import functools
import math

import jax
import jax.numpy as jnp
from jax import lax
from jax.experimental import pallas as pl
from jax.experimental.pallas import tpu as pltpu
from jax.sharding import PartitionSpec as P

NORM_EPS = 1e-05
LANES = 128
CHUNK = 512
AXES = ("gx", "gy", "gz")
F32, BF16 = jnp.float32, jnp.bfloat16
VMEM = pl.BlockSpec(memory_space=pltpu.VMEM)


def split(x):
    high = x.astype(BF16)
    low = (x - high.astype(F32)).astype(BF16)
    return jnp.concatenate([high, low], axis=1)


def dense(w):
    row = split(w)
    return jnp.concatenate([row, row], axis=0)


def halves(y):
    return y[:, :LANES] + y[:, LANES:]


def mul(a, b):
    return jnp.dot(a, b, preferred_element_type=F32)


def mul_t(a, b):
    y = lax.dot_general(a, b, (((0,), (0,)), ((), ())), preferred_element_type=F32)
    return halves(y[:LANES] + y[LANES:])


def hot(mask):
    return jnp.where(mask, 1.0, 0.0).astype(BF16)


def pick_rows(idx_row, blocks):
    col = jnp.broadcast_to(idx_row, (LANES, LANES)).T
    lane = lax.broadcasted_iota(jnp.int32, (LANES, LANES), 1)
    return jnp.concatenate([hot(col == lane + LANES * k) for k in range(blocks)], axis=1)


def pick_cols(idx_ref, tile, blocks):
    row = lax.broadcasted_iota(jnp.int32, (LANES, LANES), 0) + LANES * tile
    return jnp.concatenate(
        [hot(jnp.broadcast_to(idx_ref[b : b + 1, :], (LANES, LANES)) == row) for b in range(blocks)],
        axis=1,
    )


def centre(x):
    return x - jnp.mean(x, axis=-1, keepdims=True)


def pack_kernel(feat_ref, rows_ref, out_ref):
    table = split(feat_ref[...])
    cells = feat_ref.shape[0]
    for b in range(rows_ref.shape[0]):
        one = pick_rows(rows_ref[b : b + 1, :], cells // LANES)
        out_ref[b * LANES : (b + 1) * LANES, :] = halves(mul(one, table))


def collect_kernel(own_ref, back_ref, rows_ref, out_ref):
    grads = split(back_ref[...])
    for t in range(own_ref.shape[0] // LANES):
        at = slice(t * LANES, (t + 1) * LANES)
        out_ref[at, :] = own_ref[at, :] + halves(mul(pick_cols(rows_ref, t, rows_ref.shape[0]), grads))


def layer_kernel(
    scale,
    feat_ref, halo_ref, edge_ref, ncot_ref, ecot_ref, snd_ref, rcv_ref, cnt_ref,
    ein_ref, ebias_ref, eout_ref, egain_ref, nin_ref, nbias_ref, nout_ref, ngain_ref,
    own_ref, slot_ref, egrad_ref, wgrad_ref,
    table, both, edge_hl, hid_hl, dsilu_s, xhat_s, rstd_s, msg_hl, dout_hl, dpre_hl, up_s, recv_s,
):
    cells, halo = feat_ref.shape[0], halo_ref.shape[0]
    edges = edge_ref.shape[0]
    tbl = cells + halo
    sub = CHUNK // LANES
    eblocks = edges // LANES
    ein = ein_ref[...]
    w_e, w_s, w_r = ein[:LANES], ein[LANES : 2 * LANES], ein[2 * LANES :]
    eoc = centre(eout_ref[...])
    gain, bias = egain_ref[...], ebias_ref[...]

    table[:cells, :] = split(feat_ref[...])
    table[cells:, :] = split(halo_ref[...])
    both[:tbl, :] = split(halves(mul(table[...], dense(w_s))))
    both[tbl:, :] = split(halves(mul(table[:cells, :], dense(w_r))))
    we_cat, wo_cat = dense(w_e), dense(eoc)

    def valid_of(c):
        row = lax.broadcasted_iota(jnp.int32, (LANES, LANES), 0)
        return jnp.concatenate([jnp.where(row < cnt_ref[c * sub + k], 1.0, 0.0) for k in range(sub)], axis=0)

    def rcv_rows(c):
        return jnp.concatenate(
            [pick_rows(rcv_ref[pl.ds(c * sub + k, 1), :], cells // LANES) for k in range(sub)], axis=0
        )

    def forward(c, carry):
        at = pl.ds(pl.multiple_of(c * CHUNK, CHUNK), CHUNK)
        one = jnp.concatenate(
            [pick_rows(snd_ref[pl.ds(c * sub + k, 1), :], tbl // LANES) for k in range(sub)], axis=0
        )
        one = jnp.concatenate([one, rcv_rows(c)], axis=1)
        feat = split(edge_ref[at, :])
        edge_hl[at, :] = feat
        pre = halves(mul(one, both[...]) + mul(feat, we_cat)) + bias
        sig = jax.nn.sigmoid(pre)
        hid = pre * sig
        dsilu_s[at, :] = sig + hid * (1.0 - sig)
        hid = split(hid)
        hid_hl[at, :] = hid
        out = halves(mul(hid, wo_cat))
        rstd = lax.rsqrt(jnp.mean(out * out, axis=-1, keepdims=True) + NORM_EPS)
        xhat = out * rstd
        rstd_s[at, :] = jnp.broadcast_to(rstd, out.shape)
        xhat_s[at, :] = xhat
        msg_hl[at, :] = split(xhat * gain * valid_of(c))
        return carry

    lax.fori_loop(0, edges // CHUNK, forward, 0)

    summed = jnp.concatenate(
        [halves(mul(pick_cols(rcv_ref, t, eblocks), msg_hl[...])) for t in range(cells // LANES)], axis=0
    )
    nin, ngain = nin_ref[...], ngain_ref[...]
    noc = centre(nout_ref[...])
    feat_hl, sum_hl = table[:cells, :], split(summed)
    pre = halves(mul(feat_hl, dense(nin[:LANES])) + mul(sum_hl, dense(nin[LANES:]))) + nbias_ref[...]
    sig = jax.nn.sigmoid(pre)
    hid = pre * sig
    dsilu = sig + hid * (1.0 - sig)
    hid = split(hid)
    out = halves(mul(hid, dense(noc)))
    rstd = lax.rsqrt(jnp.mean(out * out, axis=-1, keepdims=True) + NORM_EPS)
    xhat = out * rstd
    ncot = ncot_ref[...]
    dn = ncot * ngain
    dout = split(rstd * (dn - xhat * jnp.mean(dn * xhat, axis=-1, keepdims=True)))
    dpre = halves(mul(dout, dense(noc.T))) * dsilu
    dpre_n = split(dpre)
    own_ref[...] = ncot + halves(mul(dpre_n, dense(nin[:LANES].T)))
    dsum = split(halves(mul(dpre_n, dense(nin[LANES:].T))))
    wgrad_ref[512:640, :] = mul_t(feat_hl, dpre_n) * scale
    wgrad_ref[640:768, :] = mul_t(sum_hl, dpre_n) * scale
    wgrad_ref[768:896, :] = centre(mul_t(hid, dout)) * scale
    nbias_g = jnp.sum(dpre, axis=0, keepdims=True)
    ngain_g = jnp.sum(ncot * xhat, axis=0, keepdims=True)

    wot_cat, wet_cat = dense(eoc.T), dense(w_e.T)

    def backward(c, carry):
        bias_g, gain_g = carry
        at = pl.ds(pl.multiple_of(c * CHUNK, CHUNK), CHUNK)
        ecot = ecot_ref[at, :]
        xhat = xhat_s[at, :]
        dm = (ecot + halves(mul(rcv_rows(c), dsum))) * valid_of(c)
        dn = dm * gain
        dout = split(rstd_s[at, :] * (dn - xhat * jnp.mean(dn * xhat, axis=-1, keepdims=True)))
        dout_hl[at, :] = dout
        dpre = halves(mul(dout, wot_cat)) * dsilu_s[at, :]
        dpre_c = split(dpre)
        dpre_hl[at, :] = dpre_c
        egrad_ref[at, :] = ecot + halves(mul(dpre_c, wet_cat))
        fold = lambda x: jnp.sum(x.reshape(CHUNK // 8, 8, LANES), axis=0)
        return bias_g + fold(dpre), gain_g + fold(dm * xhat)

    zero = jnp.zeros((8, LANES), F32)
    ebias_g, egain_g = lax.fori_loop(0, edges // CHUNK, backward, (zero, zero))

    wgrad_ref[384:512, :] = centre(mul_t(hid_hl[...], dout_hl[...])) * scale
    wgrad_ref[0:128, :] = mul_t(edge_hl[...], dpre_hl[...]) * scale
    wgrad_ref[896:904, :] = jnp.concatenate(
        [
            jnp.sum(ebias_g, axis=0, keepdims=True),
            jnp.sum(egain_g, axis=0, keepdims=True),
            nbias_g,
            ngain_g,
            jnp.zeros((4, LANES), F32),
        ],
        axis=0,
    ) * scale

    def up(t, carry):
        out = pl.ds(pl.multiple_of(t * LANES, LANES), LANES)
        up_s[out, :] = split(halves(mul(pick_cols(snd_ref, t, eblocks), dpre_hl[...])))
        return carry

    lax.fori_loop(0, tbl // LANES, up, 0)

    def down(t, carry):
        out = pl.ds(pl.multiple_of(t * LANES, LANES), LANES)
        recv_s[out, :] = split(halves(mul(pick_cols(rcv_ref, t, eblocks), dpre_hl[...])))
        return carry

    lax.fori_loop(0, cells // LANES, down, 0)

    wst = dense(w_s.T)
    own_ref[...] += halves(mul(up_s[:cells, :], wst) + mul(recv_s[...], dense(w_r.T)))
    slot_ref[...] = halves(mul(up_s[cells:, :], wst))
    wgrad_ref[128:256, :] = mul_t(table[...], up_s[...]) * scale
    wgrad_ref[256:384, :] = mul_t(table[:cells, :], recv_s[...]) * scale


def swap(value):
    for dim, axis in enumerate(AXES):
        peers = lax.axis_size(axis)
        up = [(i, i + 1) for i in range(peers - 1)]
        down = [(j, i) for i, j in up]
        low = lax.slice_in_dim(value, 0, 1, axis=dim)
        mid = lax.slice_in_dim(value, 1, 2, axis=dim)
        high = lax.slice_in_dim(value, 2, 3, axis=dim)
        before = lax.ppermute(high, axis, up)
        after = lax.ppermute(low, axis, down)
        value = jnp.concatenate([before, mid, after], axis=dim)
    return value


def on_device(
    node_feat, edge_feat, node_cot, edge_cot, sender, receiver, block_count, send_rows,
    edge_in_weight, edge_bias, edge_out_weight, edge_gain,
    node_in_weight, node_bias, node_out_weight, node_gain,
):
    cells, width = node_feat.shape
    edges = edge_feat.shape[0]
    slots = send_rows.shape[3]
    total = lax.axis_size("gx") * lax.axis_size("gy") * lax.axis_size("gz") * edges
    scale = 1.0 / math.sqrt(total)
    halo = -(-27 * slots // LANES) * LANES
    rows = jnp.where((jnp.arange(27) != 13)[:, None], send_rows.reshape(27, slots), -1).reshape(27 * slots)
    rows = jnp.pad(rows, (0, halo - 27 * slots), constant_values=-1).reshape(halo // LANES, LANES)

    def exchange(x):
        y = swap(x[: 27 * slots].reshape(3, 3, 3, slots, width)).reshape(27 * slots, width)
        return jnp.pad(y, ((0, halo - 27 * slots), (0, 0)))

    packets = pl.pallas_call(
        pack_kernel, out_shape=jax.ShapeDtypeStruct((halo, width), F32), in_specs=[VMEM] * 2, out_specs=VMEM,
        name="pack",
    )(node_feat, rows)
    received = exchange(packets)
    tbl = cells + halo
    big = lambda dtype, cols: pltpu.VMEM((edges, cols), dtype)
    own, slot, edge_grad, wgrad = pl.pallas_call(
        functools.partial(layer_kernel, scale),
        out_shape=(
            jax.ShapeDtypeStruct((cells, width), F32),
            jax.ShapeDtypeStruct((halo, width), F32),
            jax.ShapeDtypeStruct((edges, width), F32),
            jax.ShapeDtypeStruct((904, width), F32),
        ),
        in_specs=[VMEM] * 7 + [pl.BlockSpec(memory_space=pltpu.SMEM)] + [VMEM] * 8,
        out_specs=(VMEM,) * 4,
        scratch_shapes=[
            pltpu.VMEM((tbl, 256), BF16),
            pltpu.VMEM((tbl + cells, 256), BF16),
            big(BF16, 256),
            big(BF16, 256),
            big(F32, 128),
            big(F32, 128),
            big(F32, 128),
            big(BF16, 256),
            big(BF16, 256),
            big(BF16, 256),
            pltpu.VMEM((tbl, 256), BF16),
            pltpu.VMEM((cells, 256), BF16),
        ],
        compiler_params=pltpu.CompilerParams(vmem_limit_bytes=48 * 1024 * 1024),
        name="layer",
    )(
        node_feat, received, edge_feat, node_cot, edge_cot,
        sender.reshape(edges // LANES, LANES), receiver.reshape(edges // LANES, LANES), block_count,
        edge_in_weight, edge_bias.reshape(1, width), edge_out_weight, edge_gain.reshape(1, width),
        node_in_weight, node_bias.reshape(1, width), node_out_weight, node_gain.reshape(1, width),
    )
    total_grad = lax.psum(wgrad, AXES)
    back = exchange(slot)
    node_grad = pl.pallas_call(
        collect_kernel, out_shape=jax.ShapeDtypeStruct((cells, width), F32), in_specs=[VMEM] * 3, out_specs=VMEM,
        name="collect",
    )(own, back, rows)
    return (
        node_grad, edge_grad,
        total_grad[0:384], total_grad[896], total_grad[384:512], total_grad[897],
        total_grad[512:768], total_grad[898], total_grad[768:896], total_grad[899],
    )


def solution(mesh):
    part = P(AXES, None)
    flat = P(AXES)
    return jax.shard_map(
        on_device,
        mesh=mesh,
        in_specs=(part,) * 4 + (flat,) * 3 + (P("gx", "gy", "gz", None),) + (P(),) * 8,
        out_specs=(part,) * 2 + (P(),) * 8,
        check_vma=False,
    )
```

time: 362 us -> 221 us (0.61)
  other arithmetic: 60.9 us -> 0.19 us
  blocking collectives: 43.6 us -> 0 us
  matrix products: 35.6 us -> 0 us
  Pallas kernels: 0 us -> 22.3 us
  local copies, waits for them, and re-layouts: 33.6 us -> 11.3 us
    scatter-add x4 -> x0, other arithmetic: 44.7 us -> none  [the longest x1 13.6 us: edge_section(): node_table[receiver]]
    psum x1 -> x0, blocking collectives: 43.6 us -> none  [on_device(): lax.psum((edge_grads[2], edge_grads[3], edge_grads[4], edge_grads[5], nod...]
    dot_general x21 -> x0, matrix products: 35.6 us -> none  [the longest x3 6.69 us: edge_section(): jnp.dot(node_table[sender], edge_in_weight[width:2 * width], precision=HI...]
    gather x5 -> x0, local copies, waits for them, and re-layouts: 26.9 us -> none  [the longest x2 11 us: on_device(): edge_grads = edge_pull(edge_cot + node_grads[1][receiver])]
    pallas_call x0 -> x3, Pallas kernels: none -> 22.3 us  [the longest x1 17.9 us: on_device(): pl.pallas_call(functools.partial(layer_kernel, scale), out_shape=(jax.Sha...]
    slice x4 -> x9, local copies, waits for them, and re-layouts: 0.1 us -> 5.94 us  [the longest x1 1.62 us: on_device(): total_grad[0:384]]
    mul x9 -> x0, other arithmetic: 4.46 us -> none  [the longest x1 1.62 us: on_device(): node_weights[0] * grad_scale]
    psum x1, waiting for transfers between devices: 124 us -> 120 us  [on_device(): total_grad = lax.psum(wgrad, AXES)]
  transfers between devices with their start and end apart: 13 -> 13, of which waited for: 7 -> 9; matrix products, arithmetic and copies ran while one was open for 4% -> 3% of each run, Pallas kernels for 0% -> 0%
where the time goes in v1:
time: 221 us; the launch traced here: 220 us
  waiting for transfers between devices  145 us (66%)
  starting transfers between devices  26.6 us (12%)
  Pallas kernels  22.3 us (10%)
  between operations  14.4 us (7%)
  local copies, waits for them, and re-layouts  11.3 us (5%)
    psum x1, waiting for transfers between devices, on_device(): total_grad = lax.psum(wgrad, AXES)  120 us
    ppermute x6, waiting for transfers between devices, swap(): after = lax.ppermute(low, axis, down)  21.3 us
    ppermute x6, starting transfers between devices, swap(): before = lax.ppermute(high, axis, up)  18.8 us
    pallas_call x1, Pallas kernels, on_device(): pl.pallas_call(functools.partial(layer_kernel, scale), out_shape=(jax.Sha...  17.9 us
    ppermute x6, starting transfers between devices, swap(): after = lax.ppermute(low, axis, down)  7.75 us
    ppermute x6, waiting for transfers between devices, swap(): before = lax.ppermute(high, axis, up)  4.55 us
  transfers between devices with their start and end apart: 13, of which 9 were waited for; matrix products, arithmetic and copies ran while one was open for 3% of the time, Pallas kernels for 0%

profile of v1, /device:TPU:0, one launch (start us, length us, event | category | flops | bytes accessed | tf_op | source)
XLA Modules:
  0.0 220.2 jit_solution(16427915038369202411)
XLA Ops:
  7.2 0.0 all-reduce.5.cloned.1.call-start
  7.2 0.1 broadcast_in_dim.15
  7.3 0.1 broadcast_in_dim.16
  7.4 0.8 reshape.65
  8.2 0.6 pad_bitcast_fusion.rows_ref
  8.8 2.2 pack.1
  11.0 1.1 fusion.2
  12.1 4.9 %collective-permute-start = (f32[1,3,3,32,128]{4,3,2,1,0:T(8,128)S(1)}, f32[1,3,3,32,128]{4,3,2,1,0:T(8,128)S(1)}, u32[]{:S(2)}, u32[]{:S(2)}) collective-permute-start(f32[1,3,3,32,128]{4,3,2,1,0:T(8,128)S(1)} %bitcast.37), channel_id=1, source_target_pairs={{0,16},{1,17},{2,18},{3,19},{4,20},{5,21},{6,22},{7,23},{8,24},{9,... | collective-permute-start | bytes 442376 | tf_op jit(solution)/shard_map/ppermute | solution.py:226
  17.0 1.3 collective-permute-start.1
  18.3 1.8 collective-permute-done
  20.0 4.1 %collective-permute-done.1 = f32[1,3,3,32,128]{4,3,2,1,0:T(8,128)S(1)} collective-permute-done((f32[1,3,3,32,128]{4,3,2,1,0:T(8,128)S(1)}, f32[1,3,3,32,128]{4,3,2,1,0:T(8,128)S(1)}, u32[]{:S(2)}, u32[]{:S(2)}) %collective-permute-start.1) | collective-permute-done | bytes 147488 | tf_op jit(solution)/shard_map/ppermute | solution.py:227
  24.2 1.3 collective-permute-start.2
  25.5 1.3 collective-permute-start.3
  26.8 0.0 collective-permute-done.2
  26.9 3.7 %collective-permute-done.3 = f32[3,1,3,32,128]{4,3,2,1,0:T(8,128)S(1)} collective-permute-done((f32[3,1,3,32,128]{4,3,2,1,0:T(8,128)S(1)}, f32[3,1,3,32,128]{4,3,2,1,0:T(8,128)S(1)}, u32[]{:S(2)}, u32[]{:S(2)}) %collective-permute-start.3) | collective-permute-done | bytes 147488 | tf_op jit(solution)/shard_map/ppermute | solution.py:227
  30.5 0.0 copy-start.10
  30.6 0.0 copy-start.1
  30.6 0.0 copy-start
  30.7 3.6 %collective-permute-start.4 = (f32[3,3,1,32,128]{4,3,2,1,0:T(8,128)S(1)}, f32[3,3,1,32,128]{4,3,2,1,0:T(8,128)S(1)}, u32[]{:S(2)}, u32[]{:S(2)}) collective-permute-start(f32[3,3,1,32,128]{4,3,2,1,0:T(8,128)S(1)} %get-tuple-element.36), channel_id=1, source_target_pairs={{0,1},{1,2},{2,3},{4,5},{5,6},{6,7},{8,9},{9,10},{10,11},{12,13},{... | collective-permute-start | bytes 442376 | tf_op jit(solution)/shard_map/ppermute | solution.py:226
  34.3 1.3 collective-permute-start.5
  35.6 1.3 collective-permute-done.4
  36.9 4.4 %collective-permute-done.5 = f32[3,3,1,32,128]{4,3,2,1,0:T(8,128)S(1)} collective-permute-done((f32[3,3,1,32,128]{4,3,2,1,0:T(8,128)S(1)}, f32[3,3,1,32,128]{4,3,2,1,0:T(8,128)S(1)}, u32[]{:S(2)}, u32[]{:S(2)}) %collective-permute-start.5) | collective-permute-done | bytes 147488 | tf_op jit(solution)/shard_map/ppermute | solution.py:227
  41.4 0.0 copy-start.2
  41.4 0.0 copy-start.3
  41.4 0.0 copy-start.7
  41.4 0.0 copy-start.14
  41.4 0.0 copy-start.15
  41.5 0.0 copy-start.11
  41.5 0.0 copy-start.12
  41.5 0.0 copy-start.13
  41.5 0.0 copy-done.5
  41.5 0.0 copy-done.6
  41.5 0.0 copy-done.8
  41.5 0.0 copy-done.9
  41.5 0.0 copy-done.10
  41.5 0.0 copy-done.1
  41.5 0.0 copy-done
  41.6 0.7 copy-done.2
  42.3 0.1 copy-done.3
  42.4 0.0 copy-done.7
  42.4 0.0 copy-done.14
  42.4 0.0 copy-done.15
  42.4 17.9 %layer.1 = (f32[512,128]{1,0:T(8,128)S(1)}, f32[896,128]{1,0:T(8,128)S(1)}, f32[2048,128]{1,0:T(8,128)}, f32[904,128]{1,0:T(8,128)}) custom-call(f32[512,128]{1,0:T(8,128)S(1)} %copy-done.2, f32[896,128]{1,0:T(8,128)S(1)} %pad.12.halo_ref, f32[2048,128]{1,0:T(8,128)S(1)} %copy-done, f32[512,128]{1,0:T(8,128)S(1)} %copy-done.3, f32[2048,128]{1,0:T(8,128)S(1)} %copy-done.1, ...), custom_call_target="tpu_custom_call" | custom-call | tf_op jit(solution)/shard_map/layer/pallas_call | solution.py:257
  60.3 0.7 copy-done.4
  61.0 1.4 collective-permute-start.6
  62.5 1.3 collective-permute-start.7
  63.8 0.0 all-reduce.5.cloned.1.call-update
  63.8 1.4 collective-permute-done.6
  65.2 4.7 %collective-permute-done.7 = f32[1,3,3,32,128]{4,3,2,1,0:T(8,128)S(1)} collective-permute-done((f32[1,3,3,32,128]{4,3,2,1,0:T(8,128)S(1)}, f32[1,3,3,32,128]{4,3,2,1,0:T(8,128)S(1)}, u32[]{:S(2)}, u32[]{:S(2)}) %collective-permute-start.7) | collective-permute-done | bytes 147488 | tf_op jit(solution)/shard_map/ppermute | solution.py:227
  70.0 2.9 %collective-permute-start.8 = (f32[3,1,3,32,128]{4,3,2,1,0:T(8,128)S(1)}, f32[3,1,3,32,128]{4,3,2,1,0:T(8,128)S(1)}, u32[]{:S(2)}, u32[]{:S(2)}) collective-permute-start(f32[3,1,3,32,128]{4,3,2,1,0:T(8,128)S(1)} %get-tuple-element.33), channel_id=1, source_target_pairs={{0,4},{4,8},{8,12},{1,5},{5,9},{9,13},{2,6},{6,10},{10,14},{3,7},{... | collective-permute-start | bytes 442376 | tf_op jit(solution)/shard_map/ppermute | solution.py:226
  72.9 1.3 collective-permute-start.9
  74.2 119.5 %all-reduce.5.cloned.1.call-done = f32[904,128]{1,0:T(8,128)} async-done(((f32[904,128]{1,0:T(8,128)}), f32[904,128]{1,0:T(8,128)}) %all-reduce.5.cloned.1.call-update) | async-done | bytes 462864 | tf_op jit(solution)/shard_map/psum | solution.py:289
  193.7 1.6 slice.151
  195.3 1.6 slice.155
  196.9 1.5 fusion
  198.4 0.0 collective-permute-done.8
  198.4 0.0 collective-permute-done.9
  198.5 4.7 %collective-permute-start.10 = (f32[3,3,1,32,128]{4,3,2,1,0:T(8,128)S(1)}, f32[3,3,1,32,128]{4,3,2,1,0:T(8,128)S(1)}, u32[]{:S(2)}, u32[]{:S(2)}) collective-permute-start(f32[3,3,1,32,128]{4,3,2,1,0:T(8,128)S(1)} %get-tuple-element.30), channel_id=1, source_target_pairs={{0,1},{1,2},{2,3},{4,5},{5,6},{6,7},{8,9},{9,10},{10,11},{12,13},{... | collective-permute-start | bytes 442376 | tf_op jit(solution)/shard_map/ppermute | solution.py:226
  203.2 1.3 collective-permute-start.11
  204.5 1.4 slice_bitcast_fusion
  205.9 0.0 collective-permute-done.10
  205.9 4.4 %collective-permute-done.11 = f32[3,3,1,32,128]{4,3,2,1,0:T(8,128)S(1)} collective-permute-done((f32[3,3,1,32,128]{4,3,2,1,0:T(8,128)S(1)}, f32[3,3,1,32,128]{4,3,2,1,0:T(8,128)S(1)}, u32[]{:S(2)}, u32[]{:S(2)}) %collective-permute-start.11) | collective-permute-done | bytes 147488 | tf_op jit(solution)/shard_map/ppermute | solution.py:227
  210.3 0.8 pad.13.back_ref
  211.1 2.3 %collect.1 = f32[512,128]{1,0:T(8,128)} custom-call(f32[512,128]{1,0:T(8,128)} %copy-done.4, f32[896,128]{1,0:T(8,128)} %pad.13.back_ref, s32[7,128]{1,0:T(8,128)} %pad_bitcast_fusion.rows_ref), custom_call_target="tpu_custom_call" | custom-call | tf_op jit(solution)/shard_map/collect/pallas_call | solution.py:291
  (22 shorter events, 0.4 us)
Async XLA Ops:
  7.2 186.5 %all-reduce.5.cloned.1.call-start = ((), (), s32[]{:S(2)}) async-start(), calls=%async_computation | async-start | bytes 925696 | tf_op jit(solution)/shard_map/psum | solution.py:289
  12.1 8.0 %collective-permute-start = (f32[1,3,3,32,128]{4,3,2,1,0:T(8,128)S(1)}, f32[1,3,3,32,128]{4,3,2,1,0:T(8,128)S(1)}, u32[]{:S(2)}, u32[]{:S(2)}) collective-permute-start(f32[1,3,3,32,128]{4,3,2,1,0:T(8,128)S(1)} %bitcast.37), channel_id=1, source_target_pairs={{0,16},{1,17},{2,18},{3,19},{4,20},{5,21},{6,22},{7,23},{8,24},{9,... | collective-permute-start | bytes 442376 | tf_op jit(solution)/shard_map/ppermute | solution.py:226
  17.0 7.2 %collective-permute-start.1 = (f32[1,3,3,32,128]{4,3,2,1,0:T(8,128)S(1)}, f32[1,3,3,32,128]{4,3,2,1,0:T(8,128)S(1)}, u32[]{:S(2)}, u32[]{:S(2)}) collective-permute-start(f32[1,3,3,32,128]{4,3,2,1,0:T(8,128)S(1)} %bitcast.36), channel_id=1, source_target_pairs={{16,0},{17,1},{18,2},{19,3},{20,4},{21,5},{22,6},{23,7},{24,8},{25... | collective-permute-start | bytes 442376 | tf_op jit(solution)/shard_map/ppermute | solution.py:227
  24.2 2.6 %collective-permute-start.2 = (f32[3,1,3,32,128]{4,3,2,1,0:T(8,128)S(1)}, f32[3,1,3,32,128]{4,3,2,1,0:T(8,128)S(1)}, u32[]{:S(2)}, u32[]{:S(2)}) collective-permute-start(f32[3,1,3,32,128]{4,3,2,1,0:T(8,128)S(1)} %get-tuple-element.39), channel_id=1, source_target_pairs={{0,4},{4,8},{8,12},{1,5},{5,9},{9,13},{2,6},{6,10},{10,14},{3,7},{... | collective-permute-start | bytes 442376 | tf_op jit(solution)/shard_map/ppermute | solution.py:226
  25.5 5.0 %collective-permute-start.3 = (f32[3,1,3,32,128]{4,3,2,1,0:T(8,128)S(1)}, f32[3,1,3,32,128]{4,3,2,1,0:T(8,128)S(1)}, u32[]{:S(2)}, u32[]{:S(2)}) collective-permute-start(f32[3,1,3,32,128]{4,3,2,1,0:T(8,128)S(1)} %get-tuple-element.40), channel_id=1, source_target_pairs={{4,0},{8,4},{12,8},{5,1},{9,5},{13,9},{6,2},{10,6},{14,10},{7,3},{... | collective-permute-start | bytes 442376 | tf_op jit(solution)/shard_map/ppermute | solution.py:227
  30.5 11.0 %copy-start.5 = (f32[384,128]{1,0:T(8,128)S(1)}, f32[384,128]{1,0:T(8,128)}, u32[]{:S(2)}) copy-start(f32[384,128]{1,0:T(8,128)} %ein_ref.1) | copy-start | bytes 589828
  30.5 11.0 %copy-start.6 = (f32[256,128]{1,0:T(8,128)S(1)}, f32[256,128]{1,0:T(8,128)}, u32[]{:S(2)}) copy-start(f32[256,128]{1,0:T(8,128)} %nin_ref.1) | copy-start | bytes 393220
  30.5 11.0 %copy-start.8 = (f32[128,128]{1,0:T(8,128)S(1)}, f32[128,128]{1,0:T(8,128)}, u32[]{:S(2)}) copy-start(f32[128,128]{1,0:T(8,128)} %nout_ref.1) | copy-start | bytes 196612
  30.5 11.0 %copy-start.9 = (s32[2048]{0:T(1024)S(1)}, s32[2048]{0:T(1024)}, u32[]{:S(2)}) copy-start(s32[2048]{0:T(1024)} %param.20) | copy-start | bytes 24580
  30.5 11.0 %copy-start.10 = (s32[2048]{0:T(1024)S(1)}, s32[2048]{0:T(1024)}, u32[]{:S(2)}) copy-start(s32[2048]{0:T(1024)} %param.21) | copy-start | bytes 24580
  30.6 10.9 %copy-start.1 = (f32[2048,128]{1,0:T(8,128)S(1)}, f32[2048,128]{1,0:T(8,128)}, u32[]{:S(2)}) copy-start(f32[2048,128]{1,0:T(8,128)} %ecot_ref.1) | copy-start | bytes 3145732
  30.6 10.9 %copy-start = (f32[2048,128]{1,0:T(8,128)S(1)}, f32[2048,128]{1,0:T(8,128)}, u32[]{:S(2)}) copy-start(f32[2048,128]{1,0:T(8,128)} %edge_ref.1) | copy-start | bytes 3145732
  30.7 6.3 %collective-permute-start.4 = (f32[3,3,1,32,128]{4,3,2,1,0:T(8,128)S(1)}, f32[3,3,1,32,128]{4,3,2,1,0:T(8,128)S(1)}, u32[]{:S(2)}, u32[]{:S(2)}) collective-permute-start(f32[3,3,1,32,128]{4,3,2,1,0:T(8,128)S(1)} %get-tuple-element.36), channel_id=1, source_target_pairs={{0,1},{1,2},{2,3},{4,5},{5,6},{6,7},{8,9},{9,10},{10,11},{12,13},{... | collective-permute-start | bytes 442376 | tf_op jit(solution)/shard_map/ppermute | solution.py:226
  34.3 7.0 %collective-permute-start.5 = (f32[3,3,1,32,128]{4,3,2,1,0:T(8,128)S(1)}, f32[3,3,1,32,128]{4,3,2,1,0:T(8,128)S(1)}, u32[]{:S(2)}, u32[]{:S(2)}) collective-permute-start(f32[3,3,1,32,128]{4,3,2,1,0:T(8,128)S(1)} %get-tuple-element.37), channel_id=1, source_target_pairs={{1,0},{2,1},{3,2},{5,4},{6,5},{7,6},{9,8},{10,9},{11,10},{13,12},{... | collective-permute-start | bytes 442376 | tf_op jit(solution)/shard_map/ppermute | solution.py:227
  41.4 1.0 copy-start.2
  41.4 1.0 copy-start.3
  41.4 1.0 copy-start.7
  41.4 1.0 copy-start.14
  41.4 1.0 copy-start.15
  41.5 0.9 copy-start.11
  41.5 0.9 copy-start.12
  41.5 0.9 copy-start.13
  60.3 0.7 copy-start.4
  61.0 4.2 %collective-permute-start.6 = (f32[1,3,3,32,128]{4,3,2,1,0:T(8,128)S(1)}, f32[1,3,3,32,128]{4,3,2,1,0:T(8,128)S(1)}, u32[]{:S(2)}, u32[]{:S(2)}) collective-permute-start(f32[1,3,3,32,128]{4,3,2,1,0:T(8,128)S(1)} %bitcast.35), channel_id=1, source_target_pairs={{0,16},{1,17},{2,18},{3,19},{4,20},{5,21},{6,22},{7,23},{8,24},{9,... | collective-permute-start | bytes 442376 | tf_op jit(solution)/shard_map/ppermute | solution.py:226
  62.5 7.5 %collective-permute-start.7 = (f32[1,3,3,32,128]{4,3,2,1,0:T(8,128)S(1)}, f32[1,3,3,32,128]{4,3,2,1,0:T(8,128)S(1)}, u32[]{:S(2)}, u32[]{:S(2)}) collective-permute-start(f32[1,3,3,32,128]{4,3,2,1,0:T(8,128)S(1)} %bitcast.34), channel_id=1, source_target_pairs={{16,0},{17,1},{18,2},{19,3},{20,4},{21,5},{22,6},{23,7},{24,8},{25... | collective-permute-start | bytes 442376 | tf_op jit(solution)/shard_map/ppermute | solution.py:227
  70.0 128.4 %collective-permute-start.8 = (f32[3,1,3,32,128]{4,3,2,1,0:T(8,128)S(1)}, f32[3,1,3,32,128]{4,3,2,1,0:T(8,128)S(1)}, u32[]{:S(2)}, u32[]{:S(2)}) collective-permute-start(f32[3,1,3,32,128]{4,3,2,1,0:T(8,128)S(1)} %get-tuple-element.33), channel_id=1, source_target_pairs={{0,4},{4,8},{8,12},{1,5},{5,9},{9,13},{2,6},{6,10},{10,14},{3,7},{... | collective-permute-start | bytes 442376 | tf_op jit(solution)/shard_map/ppermute | solution.py:226
  72.9 125.5 %collective-permute-start.9 = (f32[3,1,3,32,128]{4,3,2,1,0:T(8,128)S(1)}, f32[3,1,3,32,128]{4,3,2,1,0:T(8,128)S(1)}, u32[]{:S(2)}, u32[]{:S(2)}) collective-permute-start(f32[3,1,3,32,128]{4,3,2,1,0:T(8,128)S(1)} %get-tuple-element.34), channel_id=1, source_target_pairs={{4,0},{8,4},{12,8},{5,1},{9,5},{13,9},{6,2},{10,6},{14,10},{7,3},{... | collective-permute-start | bytes 442376 | tf_op jit(solution)/shard_map/ppermute | solution.py:227
  198.5 7.4 %collective-permute-start.10 = (f32[3,3,1,32,128]{4,3,2,1,0:T(8,128)S(1)}, f32[3,3,1,32,128]{4,3,2,1,0:T(8,128)S(1)}, u32[]{:S(2)}, u32[]{:S(2)}) collective-permute-start(f32[3,3,1,32,128]{4,3,2,1,0:T(8,128)S(1)} %get-tuple-element.30), channel_id=1, source_target_pairs={{0,1},{1,2},{2,3},{4,5},{5,6},{6,7},{8,9},{9,10},{10,11},{12,13},{... | collective-permute-start | bytes 442376 | tf_op jit(solution)/shard_map/ppermute | solution.py:226
  203.2 7.0 %collective-permute-start.11 = (f32[3,3,1,32,128]{4,3,2,1,0:T(8,128)S(1)}, f32[3,3,1,32,128]{4,3,2,1,0:T(8,128)S(1)}, u32[]{:S(2)}, u32[]{:S(2)}) collective-permute-start(f32[3,3,1,32,128]{4,3,2,1,0:T(8,128)S(1)} %get-tuple-element.31), channel_id=1, source_target_pairs={{1,0},{2,1},{3,2},{5,4},{6,5},{7,6},{9,8},{10,9},{11,10},{13,12},{... | collective-permute-start | bytes 442376 | tf_op jit(solution)/shard_map/ppermute | solution.py:227
Sparse Core Ops, SparseCore 0:
  63.9 129.7 all-reduce.4

commit v2 on v1

--- a/solution.py
+++ b/solution.py
@@ -11,6 +11,7 @@
 NORM_EPS = 1e-05
 LANES = 128
 CHUNK = 512
+GRAD_ROWS = 1024
 AXES = ("gx", "gy", "gz")
 F32, BF16 = jnp.float32, jnp.bfloat16
 VMEM = pl.BlockSpec(memory_space=pltpu.VMEM)
@@ -62,19 +63,242 @@
     return x - jnp.mean(x, axis=-1, keepdims=True)
 
 
-def pack_kernel(feat_ref, rows_ref, out_ref):
+def position(sizes):
+    return tuple(lax.axis_index(axis) for axis in AXES), sizes
+
+
+def directions(spot):
+    at, sizes = spot
+    for d in range(27):
+        if d == 13:
+            continue
+        step = (d // 9 - 1, d // 3 % 3 - 1, d % 3 - 1)
+        if any(n == 1 and s != 0 for n, s in zip(sizes, step)):
+            continue
+        inside = None
+        for p, n, s in zip(at, sizes, step):
+            if s:
+                ok = p > 0 if s < 0 else p < n - 1
+                inside = ok if inside is None else jnp.logical_and(inside, ok)
+        yield d, inside, tuple(p + s for p, s in zip(at, step))
+
+
+def greet_neighbours(spot, barrier):
+    for _, inside, where in directions(spot):
+
+        @pl.when(inside)
+        def _():
+            pl.semaphore_signal(barrier, inc=1, device_id=where, device_id_type=pl.DeviceIdType.MESH)
+
+    count = 1
+    for p, n in zip(*spot):
+        count = count * (1 + (p > 0).astype(jnp.int32) + (p < n - 1).astype(jnp.int32))
+    return count - 1
+
+
+def halo_copy(d, where, out, land, send, recv):
+    return pltpu.make_async_remote_copy(
+        src_ref=out.at[d], dst_ref=land.at[26 - d], send_sem=send.at[d], recv_sem=recv.at[26 - d],
+        device_id=where, device_id_type=pl.DeviceIdType.MESH,
+    )
+
+
+def halo_start(spot, out, land, send, recv):
+    for d, inside, where in directions(spot):
+
+        @pl.when(inside)
+        def _():
+            halo_copy(d, where, out, land, send, recv).start()
+
+
+def halo_wait(spot, out, land, send, recv):
+    for d, inside, where in directions(spot):
+
+        @pl.when(inside)
+        def _():
+            halo_copy(d, where, out, land, send, recv).wait_send()
+            halo_copy(26 - d, where, out, land, send, recv).wait_recv()
+
+
+def pack_kernel(sizes, feat_ref, rows_ref, out_ref, packets, land, send, recv):
+    spot = position(sizes)
+    slots = packets.shape[1]
+    land[...] = jnp.zeros_like(land)
+    barrier = pltpu.get_barrier_semaphore()
+    count = greet_neighbours(spot, barrier)
     table = split(feat_ref[...])
     cells = feat_ref.shape[0]
     for b in range(rows_ref.shape[0]):
         one = pick_rows(rows_ref[b : b + 1, :], cells // LANES)
-        out_ref[b * LANES : (b + 1) * LANES, :] = halves(mul(one, table))
-
-
-def collect_kernel(own_ref, back_ref, rows_ref, out_ref):
+        picked = halves(mul(one, table))
+        for k in range(LANES // slots):
+            d = b * (LANES // slots) + k
+            if d < 27:
+                packets[d] = picked[k * slots : (k + 1) * slots]
+    pl.semaphore_wait(barrier, count)
+    halo_start(spot, packets, land, send, recv)
+    halo_wait(spot, packets, land, send, recv)
+    out_ref[: 27 * slots, :] = land[...].reshape(27 * slots, LANES)
+    out_ref[27 * slots :, :] = jnp.zeros((out_ref.shape[0] - 27 * slots, LANES), F32)
+
+
+def factors(axis, size, whole):
+    out, stride = [], 1
+    if whole and size <= 4:
+        return [(axis, 1, size)] if size > 1 else []
+    while size % 2 == 0:
+        out.append((axis, stride, 2))
+        stride, size = 2 * stride, size // 2
+    if size > 1:
+        out.append((axis, stride, size))
+    return out
+
+
+def sum_plan(sizes, rows):
+    fx, fy, fz = factors(0, sizes[0], False), factors(1, sizes[1], False), factors(2, sizes[2], True)
+    slot = sem = 0
+    plans = []
+
+    def lay(steps, r):
+        nonlocal slot, sem
+        laid = []
+        for axis, stride, n in steps:
+            scatters = r % (8 * n) == 0
+            r = r // n if scatters else r
+            laid.append((axis, stride, n, scatters, r, slot, sem))
+            slot, sem = slot + (n - 1) * r, sem + 2 * (n - 1)
+        return laid, r
+
+    common, r = lay(fy[:1], rows)
+    part_a, end_a = lay(fy[1:] + fx + fz, r // 2)
+    part_b, end_b = lay(fx + fy[1:] + fz, r // 2)
+    return common, r, (part_a, end_a), (part_b, end_b), slot, sem
+
+
+def sum_kernel(sizes, plan, part_ref, slot_ref, total_ref, back_ref, acc, full, rbuf, packets, land, send, recv, sems, rsems):
+    spot = position(sizes)
+    at = spot[0]
+    common, r_common, (part_a, end_a), (part_b, end_b), _, _ = plan
+    slots = packets.shape[1]
+
+    def peer(step, k):
+        axis, stride, n = step[:3]
+        digit = lax.rem(at[axis] // stride, n)
+        other = lax.rem(digit + k, n)
+        where = list(at)
+        where[axis] = at[axis] + (other - digit) * stride
+        return digit, other, tuple(where)
+
+    land[...] = jnp.zeros_like(land)
+    barrier = pltpu.get_barrier_semaphore()
+    count = greet_neighbours(spot, barrier)
+    for step in common + part_a:
+        for k in range(1, step[2]):
+            pl.semaphore_signal(
+                barrier, inc=1, device_id=peer(step, k)[2], device_id_type=pl.DeviceIdType.MESH
+            )
+            count = count + 1
+    acc[...] = part_ref[...]
+    for d in range(27):
+        packets[d] = slot_ref[d * slots : (d + 1) * slots, :]
+    pl.semaphore_wait(barrier, count)
+
+    def block(ref, start, r):
+        return ref.at[pl.ds(pl.multiple_of(start, 8), r)]
+
+    def remote(src, dst, sem, where):
+        return pltpu.make_async_remote_copy(
+            src_ref=src, dst_ref=dst, send_sem=sems.at[sem], recv_sem=rsems.at[sem],
+            device_id=where, device_id_type=pl.DeviceIdType.MESH,
+        )
+
+    def scatter(step, off, begin):
+        _, _, n, scatters, r, slot, sem = step
+        digit = None
+        for k in range(1, n):
+            digit, other, where = peer(step, k)
+            src = block(acc, off + other * r if scatters else off, r)
+            copy = remote(src, rbuf.at[pl.ds(slot + (k - 1) * r, r)], sem + k - 1, where)
+            copy.start() if begin else copy.wait()
+        mine = off + digit * r if scatters else off
+        if begin:
+            return mine
+        here = pl.ds(pl.multiple_of(mine, 8), r)
+        total = acc[here, :]
+        for k in range(1, n):
+            total = total + rbuf[slot + (k - 1) * r : slot + k * r, :]
+        acc[here, :] = total
+        return mine
+
+    def gather(step, off, begin):
+        _, _, n, scatters, r, slot, sem = step
+        if not scatters:
+            return off
+        base = off
+        for k in range(1, n):
+            digit, other, where = peer(step, k)
+            base = off - digit * r
+            copy = remote(block(full, off, r), block(full, off, r), sem + n - 1 + k - 1, where)
+            if begin:
+                copy.start()
+            else:
+                copy.wait_send()
+                source = lax.rem(digit - k + n, n)
+                came = block(full, base + source * r, r)
+                remote(came, came, sem + n - 1 + k - 1, where).wait_recv()
+        return base
+
+    off = 0
+    for step in common:
+        scatter(step, off, True)
+    halo_start(spot, packets, land, send, recv)
+    for step in common:
+        off = scatter(step, off, False)
+    starts = [off, off + r_common // 2]
+    parts = [part_a, part_b]
+    for i in range(len(part_a)):
+        for j in range(2):
+            if i:
+                starts[j] = scatter(parts[j][i - 1], starts[j], False)
+            scatter(parts[j][i], starts[j], True)
+    for j, end in ((0, end_a), (1, end_b)):
+        starts[j] = scatter(parts[j][-1], starts[j], False)
+        here = pl.ds(pl.multiple_of(starts[j], 8), end)
+        full[here, :] = acc[here, :]
+        gather(parts[j][-1], starts[j], True)
+    for i in reversed(range(len(part_a))):
+        for j in range(2):
+            starts[j] = gather(parts[j][i], starts[j], False)
+            if i:
+                gather(parts[j][i - 1], starts[j], True)
+    off = starts[0]
+    for step in reversed(common):
+        copy_off = off
+        grown = (step[0], step[1], step[2], step[3], step[4], step[5], step[6])
+        gather(grown, copy_off, True)
+        off = gather(grown, copy_off, False)
+    halo_wait(spot, packets, land, send, recv)
+    total_ref[...] = full[...]
+    back_ref[: 27 * slots, :] = land[...].reshape(27 * slots, LANES)
+    back_ref[27 * slots :, :] = jnp.zeros((back_ref.shape[0] - 27 * slots, LANES), F32)
+
+
+def finish_kernel(
+    own_ref, back_ref, rows_ref, total_ref,
+    out_ref, ein_ref, ebias_ref, eout_ref, egain_ref, nin_ref, nbias_ref, nout_ref, ngain_ref,
+):
     grads = split(back_ref[...])
     for t in range(own_ref.shape[0] // LANES):
         at = slice(t * LANES, (t + 1) * LANES)
         out_ref[at, :] = own_ref[at, :] + halves(mul(pick_cols(rows_ref, t, rows_ref.shape[0]), grads))
+    ein_ref[...] = total_ref[0:384, :]
+    eout_ref[...] = total_ref[384:512, :]
+    nin_ref[...] = total_ref[512:768, :]
+    nout_ref[...] = total_ref[768:896, :]
+    ebias_ref[...] = total_ref[896:897, :]
+    egain_ref[...] = total_ref[897:898, :]
+    nbias_ref[...] = total_ref[898:899, :]
+    ngain_ref[...] = total_ref[899:900, :]
 
 
 def layer_kernel(
@@ -183,6 +407,7 @@
 
     wgrad_ref[384:512, :] = centre(mul_t(hid_hl[...], dout_hl[...])) * scale
     wgrad_ref[0:128, :] = mul_t(edge_hl[...], dpre_hl[...]) * scale
+    wgrad_ref[904:, :] = jnp.zeros((wgrad_ref.shape[0] - 904, LANES), F32)
     wgrad_ref[896:904, :] = jnp.concatenate(
         [
             jnp.sum(ebias_g, axis=0, keepdims=True),
@@ -213,20 +438,6 @@
     slot_ref[...] = halves(mul(up_s[cells:, :], wst))
     wgrad_ref[128:256, :] = mul_t(table[...], up_s[...]) * scale
     wgrad_ref[256:384, :] = mul_t(table[:cells, :], recv_s[...]) * scale
-
-
-def swap(value):
-    for dim, axis in enumerate(AXES):
-        peers = lax.axis_size(axis)
-        up = [(i, i + 1) for i in range(peers - 1)]
-        down = [(j, i) for i, j in up]
-        low = lax.slice_in_dim(value, 0, 1, axis=dim)
-        mid = lax.slice_in_dim(value, 1, 2, axis=dim)
-        high = lax.slice_in_dim(value, 2, 3, axis=dim)
-        before = lax.ppermute(high, axis, up)
-        after = lax.ppermute(low, axis, down)
-        value = jnp.concatenate([before, mid, after], axis=dim)
-    return value
 
 
 def on_device(
@@ -243,15 +454,17 @@
     rows = jnp.where((jnp.arange(27) != 13)[:, None], send_rows.reshape(27, slots), -1).reshape(27 * slots)
     rows = jnp.pad(rows, (0, halo - 27 * slots), constant_values=-1).reshape(halo // LANES, LANES)
 
-    def exchange(x):
-        y = swap(x[: 27 * slots].reshape(3, 3, 3, slots, width)).reshape(27 * slots, width)
-        return jnp.pad(y, ((0, halo - 27 * slots), (0, 0)))
-
-    packets = pl.pallas_call(
-        pack_kernel, out_shape=jax.ShapeDtypeStruct((halo, width), F32), in_specs=[VMEM] * 2, out_specs=VMEM,
+    sizes = tuple(lax.axis_size(axis) for axis in AXES)
+    link = [pltpu.VMEM((27, slots, width), F32)] * 2 + [pltpu.SemaphoreType.DMA((27,))] * 2
+    received = pl.pallas_call(
+        functools.partial(pack_kernel, sizes),
+        out_shape=jax.ShapeDtypeStruct((halo, width), F32),
+        in_specs=[VMEM] * 2,
+        out_specs=VMEM,
+        scratch_shapes=link,
+        compiler_params=pltpu.CompilerParams(collective_id=0, has_side_effects=True),
         name="pack",
     )(node_feat, rows)
-    received = exchange(packets)
     tbl = cells + halo
     big = lambda dtype, cols: pltpu.VMEM((edges, cols), dtype)
     own, slot, edge_grad, wgrad = pl.pallas_call(
@@ -260,7 +473,7 @@
             jax.ShapeDtypeStruct((cells, width), F32),
             jax.ShapeDtypeStruct((halo, width), F32),
             jax.ShapeDtypeStruct((edges, width), F32),
-            jax.ShapeDtypeStruct((904, width), F32),
+            jax.ShapeDtypeStruct((GRAD_ROWS, width), F32),
         ),
         in_specs=[VMEM] * 7 + [pl.BlockSpec(memory_space=pltpu.SMEM)] + [VMEM] * 8,
         out_specs=(VMEM,) * 4,
@@ -286,17 +499,33 @@
         edge_in_weight, edge_bias.reshape(1, width), edge_out_weight, edge_gain.reshape(1, width),
         node_in_weight, node_bias.reshape(1, width), node_out_weight, node_gain.reshape(1, width),
     )
-    total_grad = lax.psum(wgrad, AXES)
-    back = exchange(slot)
-    node_grad = pl.pallas_call(
-        collect_kernel, out_shape=jax.ShapeDtypeStruct((cells, width), F32), in_specs=[VMEM] * 3, out_specs=VMEM,
-        name="collect",
-    )(own, back, rows)
-    return (
-        node_grad, edge_grad,
-        total_grad[0:384], total_grad[896], total_grad[384:512], total_grad[897],
-        total_grad[512:768], total_grad[898], total_grad[768:896], total_grad[899],
-    )
+    plan = sum_plan(sizes, GRAD_ROWS)
+    total_grad, back = pl.pallas_call(
+        functools.partial(sum_kernel, sizes, plan),
+        out_shape=(jax.ShapeDtypeStruct((GRAD_ROWS, width), F32), jax.ShapeDtypeStruct((halo, width), F32)),
+        in_specs=[VMEM] * 2,
+        out_specs=(VMEM, VMEM),
+        scratch_shapes=[
+            pltpu.VMEM((GRAD_ROWS, width), F32),
+            pltpu.VMEM((GRAD_ROWS, width), F32),
+            pltpu.VMEM((plan[4], width), F32),
+        ]
+        + link
+        + [pltpu.SemaphoreType.DMA((plan[5],))] * 2,
+        compiler_params=pltpu.CompilerParams(collective_id=1, has_side_effects=True),
+        name="sum",
+    )(wgrad, slot)
+    line = jax.ShapeDtypeStruct((1, width), F32)
+    square = lambda r: jax.ShapeDtypeStruct((r, width), F32)
+    node_grad, ein, ebias, eout, egain, nin, nbias, nout, ngain = pl.pallas_call(
+        finish_kernel,
+        out_shape=(square(cells), square(384), line, square(128), line, square(256), line, square(128), line),
+        in_specs=[VMEM] * 4,
+        out_specs=(VMEM,) * 9,
+        name="finish",
+    )(own, back, rows, total_grad)
+    flat = lambda x: x.reshape(width)
+    return (node_grad, edge_grad, ein, flat(ebias), eout, flat(egain), nin, flat(nbias), nout, flat(ngain))
 
 
 def solution(mesh):

time: 221 us -> 71.9 us (0.33)
  waiting for transfers between devices: 145 us -> 0 us
  Pallas kernels: 22.3 us -> 60.9 us
  starting transfers between devices: 26.6 us -> 0 us
  between operations: 14.4 us -> 0.81 us
    psum x1 -> x0, waiting for transfers between devices: 120 us -> none  [on_device(): total_grad = lax.psum(wgrad, AXES)]
    pallas_call x2 -> x3, Pallas kernels: 4.44 us -> 43.1 us  [the longest x1 30.5 us: on_device(): pl.pallas_call(functools.partial(sum_kernel, sizes, plan), out_shape=(jax...]
    ppermute x12 -> x0, starting transfers between devices: 26.6 us -> none  [the longest x6 18.8 us: swap(): before = lax.ppermute(high, axis, up)]
    ppermute x12 -> x0, waiting for transfers between devices: 25.8 us -> none  [the longest x6 21.3 us: swap(): after = lax.ppermute(low, axis, down)]
    unnamed x32 -> x40, local copies, waits for them, and re-layouts: 1.58 us -> 8.91 us
    slice x9 -> x0, local copies, waits for them, and re-layouts: 5.94 us -> none  [the longest x1 1.62 us: on_device(): total_grad[0:384]]
  transfers between devices with their start and end apart: 13 -> 0, of which waited for: 9 -> 0; matrix products, arithmetic and copies ran while one was open for 3% -> 0% of each run, Pallas kernels for 0% -> 0%
where the time goes in v2:
time: 71.9 us; the launch traced here: 71.4 us
  Pallas kernels  60.9 us (85%)
  local copies, waits for them, and re-layouts  9.75 us (14%)
  between operations  0.81 us (1%)
    pallas_call x1, Pallas kernels, on_device(): pl.pallas_call(functools.partial(sum_kernel, sizes, plan), out_shape=(jax...  30.5 us
    pallas_call x1, Pallas kernels, on_device(): pl.pallas_call(functools.partial(layer_kernel, scale), out_shape=(jax.Sha...  17.7 us
    pallas_call x1, Pallas kernels, on_device(): pl.pallas_call(functools.partial(pack_kernel, sizes), out_shape=jax.Shape...  10.2 us
    unnamed x40, local copies, waits for them, and re-layouts  8.91 us
    pallas_call x1, Pallas kernels, on_device(): pl.pallas_call(finish_kernel, out_shape=(square(cells), square(384), line...  2.47 us

profile of v2, /device:TPU:0, one launch (start us, length us, event | category | flops | bytes accessed | tf_op | source)
XLA Modules:
  0.0 71.4 jit_solution(12070073840123758495)
XLA Ops:
  0.6 0.0 copy-start.19
  0.7 0.1 broadcast_in_dim.15
  0.7 0.1 broadcast_in_dim.16
  0.8 0.5 copy-done.19
  1.4 0.1 reshape.63
  1.4 0.0 copy-start.13
  1.5 0.0 copy-start.12
  1.5 0.6 pad_bitcast_fusion.rows_ref
  2.1 0.0 copy-start.3
  2.1 0.0 copy-start.6
  2.1 0.0 copy-start.8
  2.1 0.0 copy-start.14
  2.1 0.0 copy-start.15
  2.1 0.0 copy-start.16
  2.1 0.0 copy-start.17
  2.1 0.0 copy-start.18
  2.1 10.2 %pack.1.halo_ref = f32[896,128]{1,0:T(8,128)} custom-call(f32[512,128]{1,0:T(8,128)} %feat_ref.3, s32[7,128]{1,0:T(8,128)} %pad_bitcast_fusion.rows_ref), custom_call_target="tpu_custom_call" | custom-call | tf_op jit(solution)/shard_map/pack/pallas_call | solution.py:459
  12.3 0.0 copy-done.13
  12.3 0.0 copy-done.12
  12.3 0.0 copy-done.3
  12.3 0.0 copy-done.6
  12.3 0.0 copy-done.8
  12.3 0.0 copy-done.14
  12.3 0.0 copy-done.15
  12.4 0.0 copy-done.16
  12.4 0.0 copy-done.17
  12.4 0.0 copy-done.18
  12.4 0.0 copy-start
  12.4 1.0 %copy-done = f32[896,128]{1,0:T(8,128)S(1)} copy-done((f32[896,128]{1,0:T(8,128)S(1)}, f32[896,128]{1,0:T(8,128)}, u32[]{:S(2)}) %copy-start) | copy-done | bytes 458776
  13.4 0.0 copy-start.1
  13.4 1.2 %copy-done.1 = f32[2048,128]{1,0:T(8,128)S(1)} copy-done((f32[2048,128]{1,0:T(8,128)S(1)}, f32[2048,128]{1,0:T(8,128)}, u32[]{:S(2)}) %copy-start.1) | copy-done | bytes 1048600
  14.6 0.0 copy-start.2
  14.6 1.2 %copy-done.2 = f32[2048,128]{1,0:T(8,128)S(1)} copy-done((f32[2048,128]{1,0:T(8,128)S(1)}, f32[2048,128]{1,0:T(8,128)}, u32[]{:S(2)}) %copy-start.2) | copy-done | bytes 1048600
  15.9 0.0 copy-start.9
  15.9 0.9 %copy-done.9 = f32[256,128]{1,0:T(8,128)S(1)} copy-done((f32[256,128]{1,0:T(8,128)S(1)}, f32[256,128]{1,0:T(8,128)}, u32[]{:S(2)}) %copy-start.9) | copy-done | bytes 131096
  16.8 0.0 copy-start.10
  16.8 0.8 %copy-done.10 = f32[128,128]{1,0:T(8,128)S(1)} copy-done((f32[128,128]{1,0:T(8,128)S(1)}, f32[128,128]{1,0:T(8,128)}, u32[]{:S(2)}) %copy-start.10) | copy-done | bytes 65560
  17.6 0.0 copy-start.11
  17.6 0.8 %copy-done.11 = f32[128,128]{1,0:T(8,128)S(1)} copy-done((f32[128,128]{1,0:T(8,128)S(1)}, f32[128,128]{1,0:T(8,128)}, u32[]{:S(2)}) %copy-start.11) | copy-done | bytes 65560
  18.4 17.7 %layer.1 = (f32[512,128]{1,0:T(8,128)S(1)}, f32[896,128]{1,0:T(8,128)S(1)}, f32[2048,128]{1,0:T(8,128)}, f32[1024,128]{1,0:T(8,128)S(1)}) custom-call(f32[512,128]{1,0:T(8,128)S(1)} %copy-done.3, f32[896,128]{1,0:T(8,128)S(1)} %copy-done, f32[2048,128]{1,0:T(8,128)S(1)} %copy-done.1, f32[512,128]{1,0:T(8,128)S(1)} %copy-done.6, f32[2048,128]{1,0:T(8,128)S(1)} %copy-done.2, ...), custom_call_target="tpu_custom_call" | custom-call | tf_op jit(solution)/shard_map/layer/pallas_call | solution.py:470
  36.2 0.0 copy-start.4
  36.2 0.8 %copy-done.4 = f32[1024,128]{1,0:T(8,128)} copy-done((f32[1024,128]{1,0:T(8,128)}, f32[1024,128]{1,0:T(8,128)S(1)}, u32[]{:S(2)}) %copy-start.4) | copy-done | bytes 524312
  37.0 0.0 copy-start.5
  37.0 0.8 %copy-done.5 = f32[896,128]{1,0:T(8,128)} copy-done((f32[896,128]{1,0:T(8,128)}, f32[896,128]{1,0:T(8,128)S(1)}, u32[]{:S(2)}) %copy-start.5) | copy-done | bytes 458776
  37.7 0.0 copy-start.7
  37.7 0.7 copy-done.7
  38.5 30.5 %sum.1 = (f32[1024,128]{1,0:T(8,128)}, f32[896,128]{1,0:T(8,128)}) custom-call(f32[1024,128]{1,0:T(8,128)} %copy-done.4, f32[896,128]{1,0:T(8,128)} %copy-done.5), custom_call_target="tpu_custom_call" | custom-call | tf_op jit(solution)/shard_map/sum/pallas_call | solution.py:503
  69.0 2.5 %finish.1 = (f32[512,128]{1,0:T(8,128)}, f32[384,128]{1,0:T(8,128)}, f32[1,128]{1,0:T(1,128)}, f32[128,128]{1,0:T(8,128)}, f32[1,128]{1,0:T(1,128)}, /*index=5*/...) custom-call(f32[512,128]{1,0:T(8,128)} %copy-done.7, ...), custom_call_target="tpu_custom_call" | custom-call | tf_op jit(solution)/shard_map/finish/pallas_call | solution.py:520
  (2 shorter events, 0.0 us)
Async XLA Ops:
  0.6 0.7 %copy-start.19 = (s32[3,3,3,32]{3,2,1,0:T(4,128)S(1)}, s32[3,3,3,32]{3,2,1,0:T(4,128)}, u32[]{:S(2)}) copy-start(s32[3,3,3,32]{3,2,1,0:T(4,128)} %param.23) | copy-start | bytes 10372
  1.4 10.8 %copy-start.13 = (s32[2048]{0:T(1024)S(1)}, s32[2048]{0:T(1024)}, u32[]{:S(2)}) copy-start(s32[2048]{0:T(1024)} %param.21) | copy-start | bytes 24580
  1.5 10.8 %copy-start.12 = (s32[2048]{0:T(1024)S(1)}, s32[2048]{0:T(1024)}, u32[]{:S(2)}) copy-start(s32[2048]{0:T(1024)} %param.20) | copy-start | bytes 24580
  2.1 10.3 %copy-start.3 = (f32[512,128]{1,0:T(8,128)S(1)}, f32[512,128]{1,0:T(8,128)}, u32[]{:S(2)}) copy-start(f32[512,128]{1,0:T(8,128)} %feat_ref.3) | copy-start | bytes 786436
  2.1 10.3 %copy-start.6 = (f32[512,128]{1,0:T(8,128)S(1)}, f32[512,128]{1,0:T(8,128)}, u32[]{:S(2)}) copy-start(f32[512,128]{1,0:T(8,128)} %ncot_ref.1) | copy-start | bytes 786436
  2.1 10.3 %copy-start.8 = (f32[384,128]{1,0:T(8,128)S(1)}, f32[384,128]{1,0:T(8,128)}, u32[]{:S(2)}) copy-start(f32[384,128]{1,0:T(8,128)} %ein_ref.1) | copy-start | bytes 589828
  2.1 10.3 %copy-start.14 = (s32[16]{0:T(128)S(1)}, s32[16]{0:T(128)}, u32[]{:S(2)}) copy-start(s32[16]{0:T(128)} %cnt_ref.1) | copy-start | bytes 196
  2.1 10.3 %copy-start.15 = (f32[128]{0:T(128)S(1)}, f32[128]{0:T(128)}, u32[]{:S(2)}) copy-start(f32[128]{0:T(128)} %param.25) | copy-start | bytes 1540
  2.1 10.3 %copy-start.16 = (f32[128]{0:T(128)S(1)}, f32[128]{0:T(128)}, u32[]{:S(2)}) copy-start(f32[128]{0:T(128)} %param.27) | copy-start | bytes 1540
  2.1 10.3 %copy-start.17 = (f32[128]{0:T(128)S(1)}, f32[128]{0:T(128)}, u32[]{:S(2)}) copy-start(f32[128]{0:T(128)} %param.29) | copy-start | bytes 1540
  2.1 10.3 %copy-start.18 = (f32[128]{0:T(128)S(1)}, f32[128]{0:T(128)}, u32[]{:S(2)}) copy-start(f32[128]{0:T(128)} %param.31) | copy-start | bytes 1540
  12.4 1.0 %copy-start = (f32[896,128]{1,0:T(8,128)S(1)}, f32[896,128]{1,0:T(8,128)}, u32[]{:S(2)}) copy-start(f32[896,128]{1,0:T(8,128)} %pack.1.halo_ref) | copy-start | bytes 1376260
  13.4 1.2 %copy-start.1 = (f32[2048,128]{1,0:T(8,128)S(1)}, f32[2048,128]{1,0:T(8,128)}, u32[]{:S(2)}) copy-start(f32[2048,128]{1,0:T(8,128)} %edge_ref.1) | copy-start | bytes 3145732
  14.6 1.2 %copy-start.2 = (f32[2048,128]{1,0:T(8,128)S(1)}, f32[2048,128]{1,0:T(8,128)}, u32[]{:S(2)}) copy-start(f32[2048,128]{1,0:T(8,128)} %ecot_ref.1) | copy-start | bytes 3145732
  15.9 0.9 %copy-start.9 = (f32[256,128]{1,0:T(8,128)S(1)}, f32[256,128]{1,0:T(8,128)}, u32[]{:S(2)}) copy-start(f32[256,128]{1,0:T(8,128)} %nin_ref.1) | copy-start | bytes 393220
  16.8 0.8 %copy-start.10 = (f32[128,128]{1,0:T(8,128)S(1)}, f32[128,128]{1,0:T(8,128)}, u32[]{:S(2)}) copy-start(f32[128,128]{1,0:T(8,128)} %eout_ref.1) | copy-start | bytes 196612
  17.6 0.8 %copy-start.11 = (f32[128,128]{1,0:T(8,128)S(1)}, f32[128,128]{1,0:T(8,128)}, u32[]{:S(2)}) copy-start(f32[128,128]{1,0:T(8,128)} %nout_ref.1) | copy-start | bytes 196612
  36.2 0.8 %copy-start.4 = (f32[1024,128]{1,0:T(8,128)}, f32[1024,128]{1,0:T(8,128)S(1)}, u32[]{:S(2)}) copy-start(f32[1024,128]{1,0:T(8,128)S(1)} %get-tuple-element.26.part_ref) | copy-start | bytes 1572868
  37.0 0.8 %copy-start.5 = (f32[896,128]{1,0:T(8,128)}, f32[896,128]{1,0:T(8,128)S(1)}, u32[]{:S(2)}) copy-start(f32[896,128]{1,0:T(8,128)S(1)} %get-tuple-element.27.slot_ref) | copy-start | bytes 1376260
  37.7 0.7 copy-start.7

commit v3 on v1

v3 whole, which is shorter than its diff:
```python
import functools
import math

import jax
import jax.numpy as jnp
from jax import lax
from jax.experimental import pallas as pl
from jax.experimental.pallas import tpu as pltpu
from jax.sharding import PartitionSpec as P

NORM_EPS = 1e-05
LANES = 128
CHUNK = 512
AXES = ("gx", "gy", "gz")
F32, BF16 = jnp.float32, jnp.bfloat16
VMEM = pl.BlockSpec(memory_space=pltpu.VMEM)


def split(x):
    high = x.astype(BF16)
    low = (x - high.astype(F32)).astype(BF16)
    return jnp.concatenate([high, low], axis=1)


def dense(w):
    row = split(w)
    return jnp.concatenate([row, row], axis=0)


def halves(y):
    return y[:, :LANES] + y[:, LANES:]


def mul(a, b):
    return jnp.dot(a, b, preferred_element_type=F32)


def mul_t(a, b):
    y = lax.dot_general(a, b, (((0,), (0,)), ((), ())), preferred_element_type=F32)
    return halves(y[:LANES] + y[LANES:])


def hot(mask):
    return jnp.where(mask, 1.0, 0.0).astype(BF16)


def pick_rows(idx_row, blocks):
    col = jnp.broadcast_to(idx_row, (LANES, LANES)).T
    lane = lax.broadcasted_iota(jnp.int32, (LANES, LANES), 1)
    return jnp.concatenate([hot(col == lane + LANES * k) for k in range(blocks)], axis=1)


def pick_cols(idx_ref, tile, blocks):
    row = lax.broadcasted_iota(jnp.int32, (LANES, LANES), 0) + LANES * tile
    return jnp.concatenate(
        [hot(jnp.broadcast_to(idx_ref[b : b + 1, :], (LANES, LANES)) == row) for b in range(blocks)],
        axis=1,
    )


def centre(x):
    return x - jnp.mean(x, axis=-1, keepdims=True)


def position(sizes):
    return tuple(lax.axis_index(axis) for axis in AXES), sizes


def directions(spot):
    at, sizes = spot
    for d in range(27):
        if d == 13:
            continue
        step = (d // 9 - 1, d // 3 % 3 - 1, d % 3 - 1)
        if any(n == 1 and s != 0 for n, s in zip(sizes, step)):
            continue
        inside = None
        for p, n, s in zip(at, sizes, step):
            if s:
                ok = p > 0 if s < 0 else p < n - 1
                inside = ok if inside is None else jnp.logical_and(inside, ok)
        yield d, inside, tuple(p + s for p, s in zip(at, step))


def greet_neighbours(spot, barrier):
    for _, inside, where in directions(spot):

        @pl.when(inside)
        def _():
            pl.semaphore_signal(barrier, inc=1, device_id=where, device_id_type=pl.DeviceIdType.MESH)

    count = 1
    for p, n in zip(*spot):
        count = count * (1 + (p > 0).astype(jnp.int32) + (p < n - 1).astype(jnp.int32))
    return count - 1


def halo_copy(d, where, out, land, send, recv):
    return pltpu.make_async_remote_copy(
        src_ref=out.at[d], dst_ref=land.at[26 - d], send_sem=send.at[d], recv_sem=recv.at[26 - d],
        device_id=where, device_id_type=pl.DeviceIdType.MESH,
    )


def halo_start(spot, out, land, send, recv):
    for d, inside, where in directions(spot):

        @pl.when(inside)
        def _():
            halo_copy(d, where, out, land, send, recv).start()


def halo_wait(spot, out, land, send, recv):
    for d, inside, where in directions(spot):

        @pl.when(inside)
        def _():
            halo_copy(d, where, out, land, send, recv).wait_send()
            halo_copy(26 - d, where, out, land, send, recv).wait_recv()


def sum_plan(sizes, rows, slot, sem):
    bits = []
    for axis in (1, 0, 2):
        stride = 1
        while stride < sizes[axis]:
            bits.append((axis, stride))
            stride *= 2
    groups = [bits[:1]] + [bits[i : i + 2] for i in range(1, len(bits), 2)]
    steps, r = [], rows
    for group in groups:
        n = 2 ** len(group)
        scatters = r > 64 and r % (8 * n) == 0
        r = r // n if scatters else r
        steps.append((tuple(group), scatters, r, slot, sem))
        slot, sem = slot + (n - 1) * r, sem + 2 * (n - 1)
    return steps, slot, sem


def peers_of(at, group):
    own = [lax.rem(at[axis] // stride, 2) for axis, stride in group]
    digit = sum(b * 2**i for i, b in enumerate(own))
    others = []
    for k in range(1, 2 ** len(group)):
        where, other = list(at), 0
        for i, (axis, stride) in enumerate(group):
            bit = own[i]
            if k >> i & 1:
                where[axis] = where[axis] + (1 - 2 * bit) * stride
                bit = 1 - bit
            other = other + bit * 2**i
        others.append((k, other, tuple(where)))
    return digit, others


def summing(at, steps, acc, full, rbuf, sems, rsems):
    def block(ref, start, r):
        return ref.at[pl.ds(pl.multiple_of(start, 8), r)]

    def remote(src, dst, sem, where):
        return pltpu.make_async_remote_copy(
            src_ref=src, dst_ref=dst, send_sem=sems.at[sem], recv_sem=rsems.at[sem],
            device_id=where, device_id_type=pl.DeviceIdType.MESH,
        )

    off = 0
    for group, scatters, r, slot, sem in steps:
        digit, others = peers_of(at, group)
        copies = [
            remote(
                block(acc, off + other * r if scatters else off, r),
                rbuf.at[pl.ds(slot + (k - 1) * r, r)], sem + k - 1, where,
            )
            for k, other, where in others
        ]
        for copy in copies:
            copy.start()
        yield
        for copy in copies:
            copy.wait()
        off = off + digit * r if scatters else off
        here = pl.ds(pl.multiple_of(off, 8), r)
        terms = [acc[here, :]] + [rbuf[slot + k * r : slot + (k + 1) * r, :] for k in range(len(others))]
        while len(terms) > 1:
            terms = [terms[i] + terms[i + 1] for i in range(0, len(terms), 2)]
        acc[here, :] = terms[0]
    last = steps[-1][2]
    here = pl.ds(pl.multiple_of(off, 8), last)
    full[here, :] = acc[here, :]
    for group, scatters, r, slot, sem in reversed(steps):
        if not scatters:
            continue
        digit, others = peers_of(at, group)
        base = off - digit * r
        first = sem + len(others) - 1
        for k, other, where in others:
            remote(block(full, off, r), block(full, off, r), first + k, where).start()
        yield
        for k, other, where in others:
            remote(block(full, off, r), block(full, off, r), first + k, where).wait_send()
            came = block(full, base + other * r, r)
            remote(came, came, first + k, where).wait_recv()
        off = base


def advance(*sums):
    for one in sums:
        next(one, None)


def fused_kernel(
    sizes, plans, scale,
    feat_ref, edge_ref, ncot_ref, ecot_ref, snd_ref, rcv_ref, cnt_ref, rows_ref,
    ein_ref, ebias_ref, eout_ref, egain_ref, nin_ref, nbias_ref, nout_ref, ngain_ref,
    own_ref, egrad_ref, tot_e_ref, tot_n_ref, tot_v_ref,
    table, both, edge_f, ncot_f, ecot_f, egrad_f, edge_hl, hid_hl, dsilu_s, xhat_s, rstd_s,
    msg_hl, dout_hl, dpre_hl, up_s, recv_s,
    acc_e, acc_n, acc_v, full_e, full_n, full_v, rbuf,
    packets, land, slot_out, slot_in,
    load, store, send, recv, send2, recv2, sems, rsems,
):
    spot = position(sizes)
    at = spot[0]
    cells, edges = feat_ref.shape[0], edge_ref.shape[0]
    slots = packets.shape[1]
    halo = rows_ref.shape[0] * LANES
    tbl = cells + halo
    sub = CHUNK // LANES
    eblocks, cblocks = edges // LANES, cells // LANES
    chunks = edges // CHUNK

    loads = [
        pltpu.make_async_copy(src, dst, load.at[i])
        for i, (src, dst) in enumerate(((edge_ref, edge_f), (ncot_ref, ncot_f), (ecot_ref, ecot_f)))
    ]
    for copy in loads:
        copy.start()
    land[...] = jnp.zeros_like(land)
    slot_in[...] = jnp.zeros_like(slot_in)
    barrier = pltpu.get_barrier_semaphore()
    count = greet_neighbours(spot, barrier)
    for step in plans[0]:
        for _, _, where in peers_of(at, step[0])[1]:
            pl.semaphore_signal(barrier, inc=1, device_id=where, device_id_type=pl.DeviceIdType.MESH)
            count = count + 1

    table[:cells, :] = split(feat_ref[...])
    per = LANES // slots
    for b in range(rows_ref.shape[0]):
        picked = halves(mul(pick_rows(rows_ref[b : b + 1, :], cblocks), table[:cells, :]))
        for k in range(per):
            if b * per + k < 27:
                packets[b * per + k] = picked[k * slots : (k + 1) * slots]
    pl.semaphore_wait(barrier, count)
    halo_start(spot, packets, land, send, recv)

    ein = ein_ref[...]
    w_e, w_s, w_r = ein[:LANES], ein[LANES : 2 * LANES], ein[2 * LANES :]
    eoc = centre(eout_ref[...])
    gain, bias = egain_ref[...], ebias_ref[...]
    ws_cat, we_cat, wo_cat = dense(w_s), dense(w_e), dense(eoc)
    both[:cells, :] = split(halves(mul(table[:cells, :], ws_cat)))
    both[cells : 2 * cells, :] = split(halves(mul(table[:cells, :], dense(w_r))))
    loads[0].wait()

    def valid_of(c):
        row = lax.broadcasted_iota(jnp.int32, (LANES, LANES), 0)
        return jnp.concatenate([jnp.where(row < cnt_ref[c * sub + k], 1.0, 0.0) for k in range(sub)], axis=0)

    def picks(ref, c, low, blocks):
        return jnp.concatenate(
            [pick_rows(ref[pl.ds(c * sub + k, 1), :] - low, blocks) for k in range(sub)], axis=0
        )

    def before(c, carry):
        here = pl.ds(pl.multiple_of(c * CHUNK, CHUNK), CHUNK)
        one = jnp.concatenate([picks(snd_ref, c, 0, cblocks), picks(rcv_ref, c, 0, cblocks)], axis=1)
        feat = split(edge_f[here, :])
        edge_hl[here, :] = feat
        dsilu_s[here, :] = halves(mul(one, both[: 2 * cells, :]) + mul(feat, we_cat)) + bias
        return carry

    lax.fori_loop(0, chunks, before, 0)

    halo_wait(spot, packets, land, send, recv)
    table[cells : cells + 27 * slots, :] = split(land[...].reshape(27 * slots, LANES))
    table[cells + 27 * slots :, :] = jnp.zeros((halo - 27 * slots, 2 * LANES), BF16)
    both[2 * cells :, :] = split(halves(mul(table[cells:, :], ws_cat)))

    def forward(c, carry):
        here = pl.ds(pl.multiple_of(c * CHUNK, CHUNK), CHUNK)
        one = picks(snd_ref, c, cells, halo // LANES)
        pre = dsilu_s[here, :] + halves(mul(one, both[2 * cells :, :]))
        sig = jax.nn.sigmoid(pre)
        hid = pre * sig
        dsilu_s[here, :] = sig + hid * (1.0 - sig)
        hid = split(hid)
        hid_hl[here, :] = hid
        out = halves(mul(hid, wo_cat))
        rstd = lax.rsqrt(jnp.mean(out * out, axis=-1, keepdims=True) + NORM_EPS)
        xhat = out * rstd
        rstd_s[here, :] = jnp.broadcast_to(rstd, out.shape)
        xhat_s[here, :] = xhat
        msg_hl[here, :] = split(xhat * gain * valid_of(c))
        return carry

    lax.fori_loop(0, chunks, forward, 0)

    summed = jnp.concatenate(
        [halves(mul(pick_cols(rcv_ref, t, eblocks), msg_hl[...])) for t in range(cblocks)], axis=0
    )
    nin, ngain = nin_ref[...], ngain_ref[...]
    noc = centre(nout_ref[...])
    feat_hl, sum_hl = table[:cells, :], split(summed)
    pre = halves(mul(feat_hl, dense(nin[:LANES])) + mul(sum_hl, dense(nin[LANES:]))) + nbias_ref[...]
    sig = jax.nn.sigmoid(pre)
    hid = pre * sig
    dsilu = sig + hid * (1.0 - sig)
    hid = split(hid)
    out = halves(mul(hid, dense(noc)))
    rstd = lax.rsqrt(jnp.mean(out * out, axis=-1, keepdims=True) + NORM_EPS)
    xhat = out * rstd
    loads[1].wait()
    ncot = ncot_f[...]
    dn = ncot * ngain
    dout = split(rstd * (dn - xhat * jnp.mean(dn * xhat, axis=-1, keepdims=True)))
    dpre = halves(mul(dout, dense(noc.T))) * dsilu
    dpre_n = split(dpre)
    dsum = split(halves(mul(dpre_n, dense(nin[LANES:].T))))
    acc_n[0:128, :] = mul_t(feat_hl, dpre_n) * scale
    acc_n[128:256, :] = mul_t(sum_hl, dpre_n) * scale
    acc_n[256:384, :] = centre(mul_t(hid, dout)) * scale
    node_sum = summing(at, plans[1], acc_n, full_n, rbuf, sems, rsems)
    advance(node_sum)
    own_ref[...] = ncot + halves(mul(dpre_n, dense(nin[:LANES].T)))
    nbias_g = jnp.sum(dpre, axis=0, keepdims=True)
    ngain_g = jnp.sum(ncot * xhat, axis=0, keepdims=True)

    wot_cat, wet_cat = dense(eoc.T), dense(w_e.T)
    loads[2].wait()

    def backward(c, carry):
        bias_g, gain_g = carry
        here = pl.ds(pl.multiple_of(c * CHUNK, CHUNK), CHUNK)
        ecot = ecot_f[here, :]
        xhat = xhat_s[here, :]
        dm = (ecot + halves(mul(picks(rcv_ref, c, 0, cblocks), dsum))) * valid_of(c)
        dn = dm * gain
        dout = split(rstd_s[here, :] * (dn - xhat * jnp.mean(dn * xhat, axis=-1, keepdims=True)))
        dout_hl[here, :] = dout
        dpre = halves(mul(dout, wot_cat)) * dsilu_s[here, :]
        dpre_c = split(dpre)
        dpre_hl[here, :] = dpre_c
        egrad_f[here, :] = ecot + halves(mul(dpre_c, wet_cat))
        fold = lambda x: jnp.sum(x.reshape(CHUNK // 8, 8, LANES), axis=0)
        return bias_g + fold(dpre), gain_g + fold(dm * xhat)

    zero = jnp.zeros((8, LANES), F32)
    sums = lax.fori_loop(0, chunks // 2, backward, (zero, zero))
    advance(node_sum)
    ebias_g, egain_g = lax.fori_loop(chunks // 2, chunks, backward, sums)
    advance(node_sum)
    out_copy = pltpu.make_async_copy(egrad_f, egrad_ref, store.at[0])
    out_copy.start()

    def up(t, carry):
        out = pl.ds(pl.multiple_of(t * LANES, LANES), LANES)
        up_s[out, :] = split(halves(mul(pick_cols(snd_ref, t, eblocks), dpre_hl[...])))
        return carry

    def down(t, carry):
        out = pl.ds(pl.multiple_of(t * LANES, LANES), LANES)
        recv_s[out, :] = split(halves(mul(pick_cols(rcv_ref, t, eblocks), dpre_hl[...])))
        return carry

    wst = dense(w_s.T)
    lax.fori_loop(cblocks, tbl // LANES, up, 0)
    slot_out[...] = halves(mul(up_s[cells : cells + 27 * slots, :], wst)).reshape(27, slots, LANES)
    halo_start(spot, slot_out, slot_in, send2, recv2)
    advance(node_sum)
    lax.fori_loop(0, cblocks, up, 0)
    lax.fori_loop(0, cblocks, down, 0)
    advance(node_sum)
    acc_e[0:128, :] = mul_t(edge_hl[...], dpre_hl[...]) * scale
    acc_e[128:256, :] = mul_t(table[...], up_s[...]) * scale
    acc_e[256:384, :] = mul_t(table[:cells, :], recv_s[...]) * scale
    acc_e[384:512, :] = centre(mul_t(hid_hl[...], dout_hl[...])) * scale
    acc_v[...] = jnp.concatenate(
        [
            jnp.sum(ebias_g, axis=0, keepdims=True),
            jnp.sum(egain_g, axis=0, keepdims=True),
            nbias_g,
            ngain_g,
            jnp.zeros((4, LANES), F32),
        ],
        axis=0,
    ) * scale
    edge_sum = summing(at, plans[0], acc_e, full_e, rbuf, sems, rsems)
    vec_sum = summing(at, plans[2], acc_v, full_v, rbuf, sems, rsems)
    advance(edge_sum, vec_sum)
    for _ in range(2 * len(plans[1])):
        advance(node_sum)
    own_ref[...] += halves(mul(up_s[:cells, :], wst) + mul(recv_s[...], dense(w_r.T)))
    advance(edge_sum, vec_sum)
    halo_wait(spot, slot_out, slot_in, send2, recv2)
    back = jnp.concatenate(
        [split(slot_in[...].reshape(27 * slots, LANES)), jnp.zeros((halo - 27 * slots, 2 * LANES), BF16)], axis=0
    )
    for t in range(cblocks):
        own_ref[t * LANES : (t + 1) * LANES, :] += halves(mul(pick_cols(rows_ref, t, halo // LANES), back))
    for _ in range(2 * len(plans[0])):
        advance(edge_sum, vec_sum)
    tot_e_ref[...] = full_e[...]
    tot_n_ref[...] = full_n[...]
    tot_v_ref[...] = full_v[...]
    out_copy.wait()


def finish_kernel(
    own_ref, edge_ref, node_ref, vec_ref,
    out_ref, ein_ref, ebias_ref, eout_ref, egain_ref, nin_ref, nbias_ref, nout_ref, ngain_ref,
):
    out_ref[...] = own_ref[...]
    ein_ref[...] = edge_ref[0:384, :]
    eout_ref[...] = edge_ref[384:512, :]
    nin_ref[...] = node_ref[0:256, :]
    nout_ref[...] = node_ref[256:384, :]
    for i, ref in enumerate((ebias_ref, egain_ref, nbias_ref, ngain_ref)):
        ref[...] = vec_ref[i : i + 1, :]


def on_device(
    node_feat, edge_feat, node_cot, edge_cot, sender, receiver, block_count, send_rows,
    edge_in_weight, edge_bias, edge_out_weight, edge_gain,
    node_in_weight, node_bias, node_out_weight, node_gain,
):
    cells, width = node_feat.shape
    edges = edge_feat.shape[0]
    slots = send_rows.shape[3]
    total = lax.axis_size("gx") * lax.axis_size("gy") * lax.axis_size("gz") * edges
    scale = 1.0 / math.sqrt(total)
    halo = -(-27 * slots // LANES) * LANES
    rows = jnp.where((jnp.arange(27) != 13)[:, None], send_rows.reshape(27, slots), -1).reshape(27 * slots)
    rows = jnp.pad(rows, (0, halo - 27 * slots), constant_values=-1).reshape(halo // LANES, LANES)

    sizes = tuple(lax.axis_size(axis) for axis in AXES)
    tbl = cells + halo
    plan_e, slot, sem = sum_plan(sizes, 512, 0, 0)
    plan_n, slot, sem = sum_plan(sizes, 384, slot, sem)
    plan_v, slot, sem = sum_plan(sizes, 8, slot, sem)
    link = [pltpu.VMEM((27, slots, width), F32)] * 4
    dma = lambda n: pltpu.SemaphoreType.DMA((n,))
    big = lambda dtype, cols: pltpu.VMEM((edges, cols), dtype)
    keep = lambda r: pltpu.VMEM((r, width), F32)
    pair = lambda r: pltpu.VMEM((r, 2 * width), BF16)
    hbm = pl.BlockSpec(memory_space=pl.ANY)
    square = lambda r: jax.ShapeDtypeStruct((r, width), F32)
    own, edge_grad, tot_e, tot_n, tot_v = pl.pallas_call(
        functools.partial(fused_kernel, sizes, (plan_e, plan_n, plan_v), scale),
        out_shape=(square(cells), square(edges), square(512), square(384), square(8)),
        in_specs=[VMEM, hbm, hbm, hbm, VMEM, VMEM, pl.BlockSpec(memory_space=pltpu.SMEM), VMEM] + [VMEM] * 8,
        out_specs=(VMEM, hbm, VMEM, VMEM, VMEM),
        scratch_shapes=[
            pair(tbl), pair(tbl + cells), keep(edges), keep(cells), keep(edges), keep(edges),
            pair(edges), pair(edges), keep(edges), keep(edges), keep(edges),
            pair(edges), pair(edges), pair(edges), pair(tbl), pair(cells),
            keep(512), keep(384), keep(8), keep(512), keep(384), keep(8), keep(slot),
        ]
        + link
        + [dma(3), dma(1), dma(27), dma(27), dma(27), dma(27), dma(sem), dma(sem)],
        compiler_params=pltpu.CompilerParams(
            collective_id=0, has_side_effects=True, vmem_limit_bytes=56 * 1024 * 1024
        ),
        name="layer",
    )(
        node_feat, edge_feat, node_cot, edge_cot,
        sender.reshape(edges // LANES, LANES), receiver.reshape(edges // LANES, LANES), block_count, rows,
        edge_in_weight, edge_bias.reshape(1, width), edge_out_weight, edge_gain.reshape(1, width),
        node_in_weight, node_bias.reshape(1, width), node_out_weight, node_gain.reshape(1, width),
    )
    line = jax.ShapeDtypeStruct((1, width), F32)
    node_grad, ein, ebias, eout, egain, nin, nbias, nout, ngain = pl.pallas_call(
        finish_kernel,
        out_shape=(square(cells), square(384), line, square(128), line, square(256), line, square(128), line),
        in_specs=[VMEM] * 4,
        out_specs=(VMEM,) * 9,
        name="finish",
    )(own, tot_e, tot_n, tot_v)
    flat = lambda x: x.reshape(width)
    return (node_grad, edge_grad, ein, flat(ebias), eout, flat(egain), nin, flat(nbias), nout, flat(ngain))


def solution(mesh):
    part = P(AXES, None)
    flat = P(AXES)
    return jax.shard_map(
        on_device,
        mesh=mesh,
        in_specs=(part,) * 4 + (flat,) * 3 + (P("gx", "gy", "gz", None),) + (P(),) * 8,
        out_specs=(part,) * 2 + (P(),) * 8,
        check_vma=False,
    )
```

time: 221 us -> 54.3 us (0.25)
  waiting for transfers between devices: 145 us -> 0 us
  Pallas kernels: 22.3 us -> 49.7 us
  starting transfers between devices: 26.6 us -> 0 us
  between operations: 14.4 us -> 0.67 us
  local copies, waits for them, and re-layouts: 11.3 us -> 3.64 us
    psum x1 -> x0, waiting for transfers between devices: 120 us -> none  [on_device(): total_grad = lax.psum(wgrad, AXES)]
    pallas_call x3 -> x2, Pallas kernels: 22.3 us -> 49.7 us  [the longest x1 47.8 us: on_device(): pl.pallas_call(functools.partial(fused_kernel, sizes, (plan_e, plan_n, pl...]
    ppermute x12 -> x0, starting transfers between devices: 26.6 us -> none  [the longest x6 18.8 us: swap(): before = lax.ppermute(high, axis, up)]
    ppermute x12 -> x0, waiting for transfers between devices: 25.8 us -> none  [the longest x6 21.3 us: swap(): after = lax.ppermute(low, axis, down)]
    slice x9 -> x0, local copies, waits for them, and re-layouts: 5.94 us -> none  [the longest x1 1.62 us: on_device(): total_grad[0:384]]
  transfers between devices with their start and end apart: 13 -> 0, of which waited for: 9 -> 0; matrix products, arithmetic and copies ran while one was open for 3% -> 0% of each run, Pallas kernels for 0% -> 0%
where the time goes in v3:
time: 54.3 us; the launch traced here: 54.1 us
  Pallas kernels  49.7 us (92%)
  local copies, waits for them, and re-layouts  3.64 us (7%)
  between operations  0.67 us (1%)
    pallas_call x1, Pallas kernels, on_device(): pl.pallas_call(functools.partial(fused_kernel, sizes, (plan_e, plan_n, pl...  47.8 us
    unnamed x3, local copies, waits for them, and re-layouts  2.8 us
    pallas_call x1, Pallas kernels, on_device(): pl.pallas_call(finish_kernel, out_shape=(square(cells), square(384), line...  1.96 us

profile of v3, /device:TPU:0, one launch (start us, length us, event | category | flops | bytes accessed | tf_op | source)
XLA Modules:
  0.0 54.1 jit_solution(3396706804214393704)
XLA Ops:
  0.6 0.0 copy-start
  0.7 0.1 broadcast_in_dim.15
  0.7 0.1 broadcast_in_dim.16
  0.8 0.5 copy-done
  1.4 0.1 reshape.65
  1.5 0.6 %pad_bitcast_fusion.rows_ref = s32[7,128]{1,0:T(8,128)} fusion(s32[864]{0:T(1024)S(1)} %broadcast_select_fusion), kind=kLoop, calls=%fused_computation | loop fusion | bytes 7040 | tf_op jit(solution)/shard_map/reshape | solution.py:444
  2.1 47.8 %layer.1 = (f32[512,128]{1,0:T(8,128)}, f32[2048,128]{1,0:T(8,128)}, f32[512,128]{1,0:T(8,128)}, f32[384,128]{1,0:T(8,128)}, f32[8,128]{1,0:T(8,128)}) custom-call(f32[512,128]{1,0:T(8,128)} %feat_ref.1, f32[2048,128]{1,0:T(8,128)} %edge_ref.1, f32[512,128]{1,0:T(8,128)} %ncot_ref.1, f32[2048,128]{1,0:T(8,128)} %ecot_ref.1, s32[16,128]{1,0:T(8,128)} %bitcast.12, ...), custom_call_target="tpu_custom_call" | custom-call | tf_op jit(solution)/shard_map/layer/pallas_call | solution.py:458
  49.8 2.0 %finish.1 = (f32[512,128]{1,0:T(8,128)}, f32[384,128]{1,0:T(8,128)}, f32[1,128]{1,0:T(1,128)}, f32[128,128]{1,0:T(8,128)}, f32[1,128]{1,0:T(1,128)}, /*index=5*/...) custom-call(f32[512,128]{1,0:T(8,128)} %get-tuple-element.24.own_ref, ...), custom_call_target="tpu_custom_call" | custom-call | tf_op jit(solution)/shard_map/finish/pallas_call | solution.py:482
  51.8 2.3 %copy.27 = f32[2048,128]{1,0:T(8,128)} copy(f32[2048,128]{1,0:T(8,128)} %get-tuple-element.49) | data formatting | bytes 2097152
  (2 shorter events, 0.0 us)
Async XLA Ops:
  0.6 0.7 %copy-start = (s32[3,3,3,32]{3,2,1,0:T(4,128)S(1)}, s32[3,3,3,32]{3,2,1,0:T(4,128)}, u32[]{:S(2)}) copy-start(s32[3,3,3,32]{3,2,1,0:T(4,128)} %param.23) | copy-start | bytes 10372

commit v4 on v3

--- a/solution.py
+++ b/solution.py
@@ -126,7 +126,7 @@
         while stride < sizes[axis]:
             bits.append((axis, stride))
             stride *= 2
-    groups = [bits[:1]] + [bits[i : i + 2] for i in range(1, len(bits), 2)]
+    groups = [bits[i : i + 3] for i in range(0, len(bits), 3)]
     steps, r = [], rows
     for group in groups:
         n = 2 ** len(group)
@@ -212,10 +212,11 @@
     sizes, plans, scale,
     feat_ref, edge_ref, ncot_ref, ecot_ref, snd_ref, rcv_ref, cnt_ref, rows_ref,
     ein_ref, ebias_ref, eout_ref, egain_ref, nin_ref, nbias_ref, nout_ref, ngain_ref,
-    own_ref, egrad_ref, tot_e_ref, tot_n_ref, tot_v_ref,
+    own_ref, egrad_ref, tot_e_ref, tot_o_ref, tot_n_ref, tot_m_ref,
+    tot_ebias_ref, tot_egain_ref, tot_nbias_ref, tot_ngain_ref,
     table, both, edge_f, ncot_f, ecot_f, egrad_f, edge_hl, hid_hl, dsilu_s, xhat_s, rstd_s,
     msg_hl, dout_hl, dpre_hl, up_s, recv_s,
-    acc_e, acc_n, acc_v, full_e, full_n, full_v, rbuf,
+    acc_e, acc_t, acc_n, acc_v, full_e, full_t, full_n, full_v, rbuf,
     packets, land, slot_out, slot_in,
     load, store, send, recv, send2, recv2, sems, rsems,
 ):
@@ -306,9 +307,10 @@
 
     lax.fori_loop(0, chunks, forward, 0)
 
-    summed = jnp.concatenate(
-        [halves(mul(pick_cols(rcv_ref, t, eblocks), msg_hl[...])) for t in range(cblocks)], axis=0
-    )
+    def tall(ref, low, high):
+        return jnp.concatenate([pick_cols(ref, t, eblocks) for t in range(low, high)], axis=0)
+
+    summed = halves(mul(tall(rcv_ref, 0, cblocks), msg_hl[...]))
     nin, ngain = nin_ref[...], ngain_ref[...]
     noc = centre(nout_ref[...])
     feat_hl, sum_hl = table[:cells, :], split(summed)
@@ -330,7 +332,7 @@
     acc_n[0:128, :] = mul_t(feat_hl, dpre_n) * scale
     acc_n[128:256, :] = mul_t(sum_hl, dpre_n) * scale
     acc_n[256:384, :] = centre(mul_t(hid, dout)) * scale
-    node_sum = summing(at, plans[1], acc_n, full_n, rbuf, sems, rsems)
+    node_sum = summing(at, plans[2], acc_n, full_n, rbuf, sems, rsems)
     advance(node_sum)
     own_ref[...] = ncot + halves(mul(dpre_n, dense(nin[:LANES].T)))
     nbias_g = jnp.sum(dpre, axis=0, keepdims=True)
@@ -363,28 +365,13 @@
     out_copy = pltpu.make_async_copy(egrad_f, egrad_ref, store.at[0])
     out_copy.start()
 
-    def up(t, carry):
-        out = pl.ds(pl.multiple_of(t * LANES, LANES), LANES)
-        up_s[out, :] = split(halves(mul(pick_cols(snd_ref, t, eblocks), dpre_hl[...])))
-        return carry
-
-    def down(t, carry):
-        out = pl.ds(pl.multiple_of(t * LANES, LANES), LANES)
-        recv_s[out, :] = split(halves(mul(pick_cols(rcv_ref, t, eblocks), dpre_hl[...])))
-        return carry
-
     wst = dense(w_s.T)
-    lax.fori_loop(cblocks, tbl // LANES, up, 0)
+    up_s[cells:, :] = split(halves(mul(tall(snd_ref, cblocks, tbl // LANES), dpre_hl[...])))
     slot_out[...] = halves(mul(up_s[cells : cells + 27 * slots, :], wst)).reshape(27, slots, LANES)
     halo_start(spot, slot_out, slot_in, send2, recv2)
     advance(node_sum)
-    lax.fori_loop(0, cblocks, up, 0)
-    lax.fori_loop(0, cblocks, down, 0)
-    advance(node_sum)
     acc_e[0:128, :] = mul_t(edge_hl[...], dpre_hl[...]) * scale
-    acc_e[128:256, :] = mul_t(table[...], up_s[...]) * scale
-    acc_e[256:384, :] = mul_t(table[:cells, :], recv_s[...]) * scale
-    acc_e[384:512, :] = centre(mul_t(hid_hl[...], dout_hl[...])) * scale
+    acc_e[128:256, :] = centre(mul_t(hid_hl[...], dout_hl[...])) * scale
     acc_v[...] = jnp.concatenate(
         [
             jnp.sum(ebias_g, axis=0, keepdims=True),
@@ -396,37 +383,50 @@
         axis=0,
     ) * scale
     edge_sum = summing(at, plans[0], acc_e, full_e, rbuf, sems, rsems)
-    vec_sum = summing(at, plans[2], acc_v, full_v, rbuf, sems, rsems)
+    vec_sum = summing(at, plans[3], acc_v, full_v, rbuf, sems, rsems)
     advance(edge_sum, vec_sum)
-    for _ in range(2 * len(plans[1])):
-        advance(node_sum)
+    one = jnp.concatenate([tall(snd_ref, 0, cblocks), tall(rcv_ref, 0, cblocks)], axis=0)
+    picked = split(halves(mul(one, dpre_hl[...])))
+    up_s[:cells, :] = picked[:cells]
+    recv_s[...] = picked[cells:]
+    acc_t[0:128, :] = mul_t(table[...], up_s[...]) * scale
+    acc_t[128:256, :] = mul_t(table[:cells, :], recv_s[...]) * scale
+    table_sum = summing(at, plans[1], acc_t, full_t, rbuf, sems, rsems)
+    advance(table_sum, edge_sum, vec_sum, node_sum)
     own_ref[...] += halves(mul(up_s[:cells, :], wst) + mul(recv_s[...], dense(w_r.T)))
-    advance(edge_sum, vec_sum)
+    advance(table_sum)
     halo_wait(spot, slot_out, slot_in, send2, recv2)
     back = jnp.concatenate(
         [split(slot_in[...].reshape(27 * slots, LANES)), jnp.zeros((halo - 27 * slots, 2 * LANES), BF16)], axis=0
     )
-    for t in range(cblocks):
-        own_ref[t * LANES : (t + 1) * LANES, :] += halves(mul(pick_cols(rows_ref, t, halo // LANES), back))
+    one = jnp.concatenate([pick_cols(rows_ref, t, halo // LANES) for t in range(cblocks)], axis=0)
+    own_ref[...] += halves(mul(one, back))
     for _ in range(2 * len(plans[0])):
-        advance(edge_sum, vec_sum)
-    tot_e_ref[...] = full_e[...]
-    tot_n_ref[...] = full_n[...]
-    tot_v_ref[...] = full_v[...]
+        advance(table_sum, edge_sum, vec_sum, node_sum)
+    tot_e_ref[0:128, :] = full_e[0:128, :]
+    tot_e_ref[128:384, :] = full_t[...]
+    tot_o_ref[...] = full_e[128:256, :]
+    tot_n_ref[...] = full_n[0:256, :]
+    tot_m_ref[...] = full_n[256:384, :]
+    for i, ref in enumerate((tot_ebias_ref, tot_egain_ref, tot_nbias_ref, tot_ngain_ref)):
+        ref[...] = full_v[i : i + 1, :]
     out_copy.wait()
 
 
-def finish_kernel(
-    own_ref, edge_ref, node_ref, vec_ref,
-    out_ref, ein_ref, ebias_ref, eout_ref, egain_ref, nin_ref, nbias_ref, nout_ref, ngain_ref,
-):
-    out_ref[...] = own_ref[...]
-    ein_ref[...] = edge_ref[0:384, :]
-    eout_ref[...] = edge_ref[384:512, :]
-    nin_ref[...] = node_ref[0:256, :]
-    nout_ref[...] = node_ref[256:384, :]
-    for i, ref in enumerate((ebias_ref, egain_ref, nbias_ref, ngain_ref)):
-        ref[...] = vec_ref[i : i + 1, :]
+def finish_kernel(*refs):
+    count = (len(refs) - 1) // 2
+    sems = refs[-1]
+    copies = []
+    for src, dst in zip(refs[:count], refs[count : 2 * count]):
+        rows = src.shape[0]
+        step = max(rows // 4, 256) if rows > 256 else rows
+        for low in range(0, rows, step):
+            part = pl.ds(low, min(step, rows - low))
+            copies.append(pltpu.make_async_copy(src.at[part], dst.at[part], sems.at[len(copies)]))
+    for copy in copies:
+        copy.start()
+    for copy in copies:
+        copy.wait()
 
 
 def on_device(
@@ -445,7 +445,8 @@
 
     sizes = tuple(lax.axis_size(axis) for axis in AXES)
     tbl = cells + halo
-    plan_e, slot, sem = sum_plan(sizes, 512, 0, 0)
+    plan_e, slot, sem = sum_plan(sizes, 256, 0, 0)
+    plan_t, slot, sem = sum_plan(sizes, 256, slot, sem)
     plan_n, slot, sem = sum_plan(sizes, 384, slot, sem)
     plan_v, slot, sem = sum_plan(sizes, 8, slot, sem)
     link = [pltpu.VMEM((27, slots, width), F32)] * 4
@@ -455,16 +456,17 @@
     pair = lambda r: pltpu.VMEM((r, 2 * width), BF16)
     hbm = pl.BlockSpec(memory_space=pl.ANY)
     square = lambda r: jax.ShapeDtypeStruct((r, width), F32)
-    own, edge_grad, tot_e, tot_n, tot_v = pl.pallas_call(
-        functools.partial(fused_kernel, sizes, (plan_e, plan_n, plan_v), scale),
-        out_shape=(square(cells), square(edges), square(512), square(384), square(8)),
+    outs = (square(cells), square(edges), square(384), square(128), square(256), square(128)) + (square(1),) * 4
+    made = pl.pallas_call(
+        functools.partial(fused_kernel, sizes, (plan_e, plan_t, plan_n, plan_v), scale),
+        out_shape=outs,
         in_specs=[VMEM, hbm, hbm, hbm, VMEM, VMEM, pl.BlockSpec(memory_space=pltpu.SMEM), VMEM] + [VMEM] * 8,
-        out_specs=(VMEM, hbm, VMEM, VMEM, VMEM),
+        out_specs=(VMEM, hbm) + (VMEM,) * 8,
         scratch_shapes=[
             pair(tbl), pair(tbl + cells), keep(edges), keep(cells), keep(edges), keep(edges),
             pair(edges), pair(edges), keep(edges), keep(edges), keep(edges),
             pair(edges), pair(edges), pair(edges), pair(tbl), pair(cells),
-            keep(512), keep(384), keep(8), keep(512), keep(384), keep(8), keep(slot),
+            keep(256), keep(256), keep(384), keep(8), keep(256), keep(256), keep(384), keep(8), keep(slot),
         ]
         + link
         + [dma(3), dma(1), dma(27), dma(27), dma(27), dma(27), dma(sem), dma(sem)],
@@ -478,14 +480,14 @@
         edge_in_weight, edge_bias.reshape(1, width), edge_out_weight, edge_gain.reshape(1, width),
         node_in_weight, node_bias.reshape(1, width), node_out_weight, node_gain.reshape(1, width),
     )
-    line = jax.ShapeDtypeStruct((1, width), F32)
-    node_grad, ein, ebias, eout, egain, nin, nbias, nout, ngain = pl.pallas_call(
+    node_grad, edge_grad, ein, eout, nin, nout, ebias, egain, nbias, ngain = pl.pallas_call(
         finish_kernel,
-        out_shape=(square(cells), square(384), line, square(128), line, square(256), line, square(128), line),
-        in_specs=[VMEM] * 4,
-        out_specs=(VMEM,) * 9,
+        out_shape=outs,
+        in_specs=[hbm] * len(outs),
+        out_specs=(hbm,) * len(outs),
+        scratch_shapes=[dma(24)],
         name="finish",
-    )(own, tot_e, tot_n, tot_v)
+    )(*made)
     flat = lambda x: x.reshape(width)
     return (node_grad, edge_grad, ein, flat(ebias), eout, flat(egain), nin, flat(nbias), nout, flat(ngain))
 

time: 54.3 us -> 106 us (1.95)
  Pallas kernels: 49.7 us -> 104 us
  local copies, waits for them, and re-layouts: 3.64 us -> 1.38 us
    pallas_call x2, Pallas kernels: 49.7 us -> 104 us  [the longest x1 55 us: on_device(): pl.pallas_call(finish_kernel, out_shape=outs, in_specs=[hbm] * len(outs),...]
    unnamed x3 -> x2, local copies, waits for them, and re-layouts: 2.8 us -> 0.54 us
where the time goes in v4:
time: 106 us
  Pallas kernels  104 us (98%)
  local copies, waits for them, and re-layouts  1.38 us (1%)
    pallas_call x1, Pallas kernels, on_device(): pl.pallas_call(finish_kernel, out_shape=outs, in_specs=[hbm] * len(outs),...  55 us
    pallas_call x1, Pallas kernels, on_device(): pl.pallas_call(functools.partial(fused_kernel, sizes, (plan_e, plan_t, pl...  49.2 us

profile of v4, /device:TPU:0, one launch (start us, length us, event | category | flops | bytes accessed | tf_op | source)
XLA Modules:
  0.0 106.3 jit_solution(8552014860338021342)
XLA Ops:
  0.6 0.0 copy-start
  0.7 0.1 broadcast_in_dim.15
  0.7 0.1 broadcast_in_dim.16
  0.8 0.5 copy-done
  1.4 0.1 reshape.65
  1.5 0.6 pad_bitcast_fusion.rows_ref
  2.1 49.2 %layer.1 = (f32[512,128]{1,0:T(8,128)}, f32[2048,128]{1,0:T(8,128)}, f32[384,128]{1,0:T(8,128)}, f32[128,128]{1,0:T(8,128)}, f32[256,128]{1,0:T(8,128)}, /*index...) custom-call(f32[512,128]{1,0:T(8,128)} %feat_ref.1, ...), custom_call_target="tpu_custom_call" | custom-call | tf_op jit(solution)/shard_map/layer/pallas_call | solution.py:460
  51.3 55.0 %finish.1 = (f32[512,128]{1,0:T(8,128)}, f32[2048,128]{1,0:T(8,128)}, f32[384,128]{1,0:T(8,128)}, f32[128,128]{1,0:T(8,128)}, f32[256,128]{1,0:T(8,128)}, /*inde...) custom-call(f32[512,128]{1,0:T(8,128)} %get-tuple-element.30.refs_0_, ...), custom_call_target="tpu_custom_call" | custom-call | tf_op jit(solution)/shard_map/finish/pallas_call | solution.py:483
  (2 shorter events, 0.0 us)
Async XLA Ops:
  0.6 0.7 copy-start

commit v5 on v4

--- a/solution.py
+++ b/solution.py
@@ -126,7 +126,7 @@
         while stride < sizes[axis]:
             bits.append((axis, stride))
             stride *= 2
-    groups = [bits[i : i + 3] for i in range(0, len(bits), 3)]
+    groups = [bits[:1]] + [bits[i : i + 2] for i in range(1, len(bits), 2)]
     steps, r = [], rows
     for group in groups:
         n = 2 ** len(group)
@@ -307,10 +307,9 @@
 
     lax.fori_loop(0, chunks, forward, 0)
 
-    def tall(ref, low, high):
-        return jnp.concatenate([pick_cols(ref, t, eblocks) for t in range(low, high)], axis=0)
-
-    summed = halves(mul(tall(rcv_ref, 0, cblocks), msg_hl[...]))
+    summed = jnp.concatenate(
+        [halves(mul(pick_cols(rcv_ref, t, eblocks), msg_hl[...])) for t in range(cblocks)], axis=0
+    )
     nin, ngain = nin_ref[...], ngain_ref[...]
     noc = centre(nout_ref[...])
     feat_hl, sum_hl = table[:cells, :], split(summed)
@@ -366,7 +365,18 @@
     out_copy.start()
 
     wst = dense(w_s.T)
-    up_s[cells:, :] = split(halves(mul(tall(snd_ref, cblocks, tbl // LANES), dpre_hl[...])))
+
+    def up(t, carry):
+        out = pl.ds(pl.multiple_of(t * LANES, LANES), LANES)
+        up_s[out, :] = split(halves(mul(pick_cols(snd_ref, t, eblocks), dpre_hl[...])))
+        return carry
+
+    def down(t, carry):
+        out = pl.ds(pl.multiple_of(t * LANES, LANES), LANES)
+        recv_s[out, :] = split(halves(mul(pick_cols(rcv_ref, t, eblocks), dpre_hl[...])))
+        return carry
+
+    lax.fori_loop(cblocks, tbl // LANES, up, 0)
     slot_out[...] = halves(mul(up_s[cells : cells + 27 * slots, :], wst)).reshape(27, slots, LANES)
     halo_start(spot, slot_out, slot_in, send2, recv2)
     advance(node_sum)
@@ -385,10 +395,9 @@
     edge_sum = summing(at, plans[0], acc_e, full_e, rbuf, sems, rsems)
     vec_sum = summing(at, plans[3], acc_v, full_v, rbuf, sems, rsems)
     advance(edge_sum, vec_sum)
-    one = jnp.concatenate([tall(snd_ref, 0, cblocks), tall(rcv_ref, 0, cblocks)], axis=0)
-    picked = split(halves(mul(one, dpre_hl[...])))
-    up_s[:cells, :] = picked[:cells]
-    recv_s[...] = picked[cells:]
+    lax.fori_loop(0, cblocks, up, 0)
+    advance(edge_sum, vec_sum, node_sum)
+    lax.fori_loop(0, cblocks, down, 0)
     acc_t[0:128, :] = mul_t(table[...], up_s[...]) * scale
     acc_t[128:256, :] = mul_t(table[:cells, :], recv_s[...]) * scale
     table_sum = summing(at, plans[1], acc_t, full_t, rbuf, sems, rsems)
@@ -414,19 +423,9 @@
 
 
 def finish_kernel(*refs):
-    count = (len(refs) - 1) // 2
-    sems = refs[-1]
-    copies = []
-    for src, dst in zip(refs[:count], refs[count : 2 * count]):
-        rows = src.shape[0]
-        step = max(rows // 4, 256) if rows > 256 else rows
-        for low in range(0, rows, step):
-            part = pl.ds(low, min(step, rows - low))
-            copies.append(pltpu.make_async_copy(src.at[part], dst.at[part], sems.at[len(copies)]))
-    for copy in copies:
-        copy.start()
-    for copy in copies:
-        copy.wait()
+    count = len(refs) // 2
+    for src, dst in zip(refs[:count], refs[count:]):
+        dst[...] = src[...]
 
 
 def on_device(
@@ -483,9 +482,8 @@
     node_grad, edge_grad, ein, eout, nin, nout, ebias, egain, nbias, ngain = pl.pallas_call(
         finish_kernel,
         out_shape=outs,
-        in_specs=[hbm] * len(outs),
-        out_specs=(hbm,) * len(outs),
-        scratch_shapes=[dma(24)],
+        in_specs=[VMEM] * len(outs),
+        out_specs=(VMEM,) * len(outs),
         name="finish",
     )(*made)
     flat = lambda x: x.reshape(width)

time: 106 us -> 51.5 us (0.49)
  Pallas kernels: 104 us -> 49.2 us
    pallas_call x1, Pallas kernels: 55 us -> 2.72 us  [on_device(): pl.pallas_call(finish_kernel, out_shape=outs, in_specs=[VMEM] * len(outs)...]
    pallas_call x1, Pallas kernels: 49.2 us -> 46.5 us  [on_device(): pl.pallas_call(functools.partial(fused_kernel, sizes, (plan_e, plan_t, pl...]
where the time goes in v5:
time: 51.5 us; the launch traced here: 51.2 us
  Pallas kernels  49.2 us (96%)
  local copies, waits for them, and re-layouts  1.38 us (3%)
  between operations  0.67 us (1%)
    pallas_call x1, Pallas kernels, on_device(): pl.pallas_call(functools.partial(fused_kernel, sizes, (plan_e, plan_t, pl...  46.5 us
    pallas_call x1, Pallas kernels, on_device(): pl.pallas_call(finish_kernel, out_shape=outs, in_specs=[VMEM] * len(outs)...  2.72 us

profile of v5, /device:TPU:0, one launch (start us, length us, event | category | flops | bytes accessed | tf_op | source)
XLA Modules:
  0.0 51.2 jit_solution(1798330966105944500)
XLA Ops:
  0.6 0.0 copy-start
  0.7 0.1 broadcast_in_dim.15
  0.7 0.1 broadcast_in_dim.16
  0.8 0.5 %copy-done = s32[3,3,3,32]{3,2,1,0:T(4,128)S(1)} copy-done((s32[3,3,3,32]{3,2,1,0:T(4,128)S(1)}, s32[3,3,3,32]{3,2,1,0:T(4,128)}, u32[]{:S(2)}) %copy-start) | copy-done | bytes 3480
  1.4 0.1 reshape.65
  1.5 0.6 %pad_bitcast_fusion.rows_ref = s32[7,128]{1,0:T(8,128)} fusion(s32[864]{0:T(1024)S(1)} %broadcast_select_fusion), kind=kLoop, calls=%fused_computation | loop fusion | bytes 7040 | tf_op jit(solution)/shard_map/reshape | solution.py:443
  2.1 46.5 %layer.1 = (f32[512,128]{1,0:T(8,128)}, f32[2048,128]{1,0:T(8,128)}, f32[384,128]{1,0:T(8,128)}, f32[128,128]{1,0:T(8,128)}, f32[256,128]{1,0:T(8,128)}, /*index...) custom-call(f32[512,128]{1,0:T(8,128)} %feat_ref.1, ...), custom_call_target="tpu_custom_call" | custom-call | tf_op jit(solution)/shard_map/layer/pallas_call | solution.py:459
  48.5 2.7 %finish.1 = (f32[512,128]{1,0:T(8,128)}, f32[2048,128]{1,0:T(8,128)}, f32[384,128]{1,0:T(8,128)}, f32[128,128]{1,0:T(8,128)}, f32[256,128]{1,0:T(8,128)}, /*inde...) custom-call(f32[512,128]{1,0:T(8,128)} %get-tuple-element.30.refs_0_, ...), custom_call_target="tpu_custom_call" | custom-call | tf_op jit(solution)/shard_map/finish/pallas_call | solution.py:482
  (2 shorter events, 0.0 us)
Async XLA Ops:
  0.6 0.7 %copy-start = (s32[3,3,3,32]{3,2,1,0:T(4,128)S(1)}, s32[3,3,3,32]{3,2,1,0:T(4,128)}, u32[]{:S(2)}) copy-start(s32[3,3,3,32]{3,2,1,0:T(4,128)} %param.23) | copy-start | bytes 10372
